TPU v7x, 128 devices: a whole 4x4x4 slice. The times are simulated.
128 devices in a mesh: dp: 32 (over x, y, z_hi), space: 4 (over z_lo, core).
Axes of the slice: x: 4, y: 4, z: 4 (z_hi: 2, z_lo: 2; z = z_hi * 2 + z_lo), core: 2. Of those that a mesh axis runs over, the one named last changes fastest.
Arguments:
- features: bfloat16 [32, 8, 512, 384], P('dp', 'space'), may hold values from -6 to 6
- cotangent: bfloat16 [32, 8, 512, 384], P('dp', 'space'), may hold values from -6 to 6
- weight: bfloat16 [10368, 384], P('dp'), may hold values from -0.0625 to 0.0625
- occupancy: int32 [32, 8, 512], P('dp'), may hold values from 0 to 1, as said below
- neighbours: int32 [32, 8, 27], P('dp'), may hold values from -1 to 7, as said below
- first_moment: float32 [10368, 384], P('dp', 'space'), may hold values from -6 to 6
- second_moment: float32 [10368, 384], P('dp', 'space'), may hold values from 0.01 to 4
Outputs:
- input_grad: bfloat16 [32, 8, 512, 384], P('dp', 'space')
- new_first: float32 [10368, 384], P('dp', 'space')
- new_second: float32 [10368, 384], P('dp', 'space')
Inputs may be any that keep to these rules, and one draw needn't show every extreme that they name: `neighbours`: slots s * 2 to s * 2 + 1 of a window lie on index s of space. Exactly 4 slots of each window hold a block, slot 7 always among them, and in every window one index of space has all 2 of its slots holding one. For a slot holding a block, entry 13 is the slot itself and entry 9 e1 + 3 e2 + e3 is the slot of the block displaced by (e1 - 1, e2 - 1, e3 - 1) block widths, or -1 if no block lies there; the relation is symmetric and entries name only slots holding blocks. Every entry of an empty slot is -1. `occupancy`: zero in every slot that holds no block.
All inputs are finite; a program needn't handle non-finite values.
Results may differ from a plain program's by a relative error of at most 0.006.
Values may be sent and summed in bfloat16 or wider, within the bound.
A program may use at most 192 MiB of HBM per device.

v0:
```python
import jax
import jax.numpy as jnp
from jax import lax
from jax.sharding import PartitionSpec as P

EDGE_SPANS = ((7, 8), (0, 8), (0, 1))


def build_region(lookup, neighbour_rows):
    slab_list = []
    for first_axis in range(3):
        planes = []
        for second_axis in range(3):
            pieces = []
            for third_axis in range(3):
                offset_code = 9 * first_axis + 3 * second_axis + third_axis
                span_one = EDGE_SPANS[first_axis]
                span_two = EDGE_SPANS[second_axis]
                span_three = EDGE_SPANS[third_axis]
                window_part = lookup[
                    :,
                    span_one[0] : span_one[1],
                    span_two[0] : span_two[1],
                    span_three[0] : span_three[1],
                    :,
                ]
                pieces.append(jnp.take(window_part, neighbour_rows[:, offset_code], axis=0))
            planes.append(jnp.concatenate(pieces, axis=3))
        slab_list.append(jnp.concatenate(planes, axis=2))
    return jnp.concatenate(slab_list, axis=1)


def shifted(region, offset):
    first_axis = offset // 9
    second_axis = offset // 3 % 3
    third_axis = offset % 3
    moved = region[
        :,
        first_axis : first_axis + 8,
        second_axis : second_axis + 8,
        third_axis : third_axis + 8,
        :,
    ]
    return moved.reshape(-1, region.shape[-1])


def column_block(region, channel_count):
    stacked = jnp.stack([shifted(region, offset) for offset in range(27)], axis=2)
    return stacked.reshape(stacked.shape[0], channel_count * 27)


def body(features, cotangent, weight, occupancy, neighbours, first_moment, second_moment):
    channels = features.shape[3]
    capacity = features.shape[1]
    spatial = lax.axis_size("space")
    group_size = capacity * spatial
    position = lax.axis_index("space")
    voxel_mask = occupancy[0].astype(jnp.float32)
    neighbour_ids = neighbours[0]
    own_slots = position * capacity + jnp.arange(capacity, dtype=jnp.int32)
    handled_count = own_slots.shape[0]
    flat_rows = handled_count * 512
    whole_feat = lax.all_gather(features, "space", axis=1, tiled=True)[0]
    cot_rows = cotangent[0].reshape(flat_rows, channels).astype(jnp.float32)
    masked = whole_feat * occupancy[0][:, :, None].astype(jnp.bfloat16)
    lookup = jnp.concatenate(
        [
            masked.reshape(group_size, 8, 8, 8, channels),
            jnp.zeros((1, 8, 8, 8, channels), jnp.bfloat16),
        ],
        axis=0,
    )
    neighbour_slots = jnp.where(neighbour_ids < 0, group_size, neighbour_ids)
    region = build_region(lookup, jnp.take(neighbour_slots, own_slots, axis=0))
    mask_rows = jnp.take(voxel_mask, own_slots, axis=0).reshape(flat_rows, 1)
    weight_piece = lax.all_gather(weight, "dp", axis=0, tiled=True)
    block_cols = column_block(region, weight_piece.shape[0] // 27)
    pre = jnp.dot(block_cols, weight_piece, preferred_element_type=jnp.float32)
    weight_cube = lax.all_gather(weight, "dp", axis=0, tiled=True).reshape(channels, 27, channels)
    sigmoid_pre = jax.nn.sigmoid(pre)
    delta_rows = (cot_rows * mask_rows * sigmoid_pre * (1.0 + pre * (1.0 - sigmoid_pre))).astype(
        jnp.bfloat16
    )
    delta_blocks = delta_rows.reshape(handled_count, 512, channels)
    delta_all = lax.all_gather(delta_blocks, "space", axis=0, tiled=True)
    tail_index = delta_all.shape[0]
    delta_slots = jnp.where(neighbour_ids < 0, tail_index, neighbour_ids)
    delta_lookup = jnp.concatenate(
        [
            delta_all.reshape(tail_index, 8, 8, 8, channels),
            jnp.zeros((1, 8, 8, 8, channels), jnp.bfloat16),
        ],
        axis=0,
    )
    delta_region = build_region(delta_lookup, jnp.take(delta_slots, own_slots, axis=0))
    back_rows = jnp.zeros((flat_rows, channels), jnp.float32)
    for offset in range(27):
        back_rows = back_rows + lax.dot_general(
            shifted(delta_region, 26 - offset),
            weight_cube[:, offset, :],
            (((1,), (1,)), ((), ())),
            preferred_element_type=jnp.float32,
        )
    back_rows = mask_rows * back_rows
    own_back = back_rows.reshape(capacity, 512, channels)
    input_grad = (cotangent[0].astype(jnp.float32) + own_back).astype(jnp.bfloat16)[None]
    rows_here = 27 * channels // lax.axis_size("dp")
    block_cols = column_block(region, rows_here * lax.axis_size("dp") // 27)
    row_share = lax.psum_scatter(
        lax.dot_general(
            block_cols, delta_rows, (((0,), (0,)), ((), ())), preferred_element_type=jnp.float32
        ).astype(jnp.bfloat16),
        "dp",
        scatter_dimension=0,
        tiled=True,
    )
    summed = lax.psum_scatter(row_share, "space", scatter_dimension=1, tiled=True).astype(
        jnp.float32
    )
    scaled_grad = summed / 64.0
    new_first = 0.9 * first_moment + 0.1 * scaled_grad
    new_second = 0.999 * second_moment + 0.001 * scaled_grad * scaled_grad
    return (input_grad, new_first, new_second)


def solution(mesh):
    return jax.shard_map(
        body,
        mesh=mesh,
        in_specs=(
            P("dp", "space", None, None),
            P("dp", "space", None, None),
            P("dp", None),
            P("dp", None, None),
            P("dp", None, None),
            P("dp", "space"),
            P("dp", "space"),
        ),
        out_specs=(P("dp", "space", None, None), P("dp", "space"), P("dp", "space")),
        check_vma=False,
    )
```

profile of v0, /device:TPU:1, one launch (start us, length us, event | category | flops | bytes accessed | tf_op | source)
XLA Modules:
  0.0 707.0 jit_solution(12912879570296211923)
XLA Ops:
  29.0 22.2 %all-gather.5.cloned.1.call-done = bf16[1,8,512,384]{3,2,0,1:T(8,128)(2,1)} async-done(((bf16[1,2,512,384]{3,2,0,1:T(8,128)(2,1)}), bf16[1,8,512,384]{3,2,0,1:T(8,128)(2,1)}) %all-gather.5.cloned.1.call-update) | async-done | bytes 3145744 | tf_op jit(solution)/shard_map/all_gather | solution.py:63
  51.2 3.7 copy.172
  56.0 2.2 copy.453
  70.2 2.1 gather_fusion.11
  106.4 2.1 gather_fusion.13
  110.2 2.1 gather_fusion.17
  112.3 2.1 gather_fusion.19
  114.4 2.4 concatenate.156.clone
  116.8 2.9 gather_fusion.15
  157.6 2.5 maximum_maximum_fusion.5
  171.7 6.8 maximum_maximum_fusion.1
  188.9 31.3 %copy.216 = bf16[1024,384,27]{0,2,1:T(8,128)(2,1)} copy(bf16[1024,384,27]{1,0,2:T(8,128)(2,1)} %constant_dynamic-update-slice_fusion) | data formatting | bytes 42467328 | tf_op jit(solution)/shard_map/stack | solution.py:48
  220.2 26.7 %reshape.272 = bf16[1024,10368]{0,1:T(8,128)(2,1)} reshape(bf16[1024,384,27]{0,2,1:T(8,128)(2,1)} %copy.216) | data formatting | bytes 42467328 | tf_op jit(solution)/shard_map/reshape | solution.py:49
  247.0 9.3 %reshape.1137 = bf16[10368,384]{1,0:T(8,128)(2,1)} reshape(bf16[32,324,384]{2,1,0:T(8,128)(2,1)} %all-gather.9.cloned.1.call-done) | data formatting | bytes 15925248
  256.2 18.2 %fusion.3 = bf16[1024,384]{1,0:T(8,128)(2,1)S(1)} fusion(f32[1024]{0:T(1024)S(1)} %bitcast.499, bf16[1,2,512,384]{3,2,1,0:T(8,128)(2,1)S(1)} %copy-done.50, bf16[1024,10368]{0,1:T(8,128)(2,1)} %reshape.272, bf16[10368,384]{1,0:T(8,128)(2,1)} %reshape.1137), kind=kOutput, calls=%fused_computation.94 | convolution fusion | flops 8158052352 | bytes 30773248 | tf_op jit(solution)/shard_map/dot_general | solution.py:78
  274.5 18.0 %convolution_convert_fusion = bf16[10368,384]{1,0:T(8,128)(2,1)} fusion(bf16[1024,10368]{0,1:T(8,128)(2,1)} %reshape.272, bf16[1024,384]{1,0:T(8,128)(2,1)S(1)} %fusion.3), kind=kOutput, calls=%fused_computation.82 | convolution fusion | flops 8157708288 | bytes 29982720 | tf_op jit(solution)/shard_map/dot_general | solution.py:110
  292.5 187.1 %fusion = bf16[336,384]{1,0:T(8,128)(2,1)S(1)} fusion(bf16[10368,384]{1,0:T(8,128)(2,1)} %convolution_convert_fusion), kind=kCustom, calls=%all-reduce-scatter | all-reduce-scatter fusion | flops 4128769 | bytes 8221184
  481.1 2.7 collective-permute-start.1
  488.7 13.1 %reshape.276 = bf16[384,27,384]{2,1,0:T(8,128)(2,1)} reshape(bf16[32,324,384]{2,1,0:T(8,128)(2,1)} %all-gather.9.cloned.1.call-done) | data formatting | bytes 15925248 | tf_op jit(solution)/shard_map/reshape | solution.py:79
  501.7 12.8 %fusion.115 = (bf16[384,1,384]{2,1,0:T(2,128)(2,1)}, bf16[384,1,384]{2,1,0:T(2,128)(2,1)}, bf16[384,1,384]{2,1,0:T(2,128)(2,1)}, bf16[384,1,384]{2,1,0:T(2,128)(...) fusion(bf16[384,27,384]{2,1,0:T(8,128)(2,1)} %reshape.276), kind=kLoop, calls=%fused_computation.445 | loop fusion | bytes 4718592 | tf_op jit(solution)/shard_map/slice | solution.py:100
  514.5 10.6 %fusion.114 = (bf16[384,1,384]{2,1,0:T(2,128)(2,1)}, bf16[384,1,384]{2,1,0:T(2,128)(2,1)}, bf16[384,1,384]{2,1,0:T(2,128)(2,1)}, bf16[384,1,384]{2,1,0:T(2,128)(...) fusion(bf16[384,27,384]{2,1,0:T(8,128)(2,1)S(1)} %copy-done), kind=kLoop, calls=%fused_computation.444 | loop fusion | bytes 11206656 | tf_op jit(solution)/shard_map/slice | solution.py:100
  527.8 22.8 %all-gather.7.cloned.1.call-done = bf16[8,512,384]{2,1,0:T(8,128)(2,1)} async-done(((bf16[2,512,384]{2,1,0:T(8,128)(2,1)}), bf16[8,512,384]{2,1,0:T(8,128)(2,1)}) %all-gather.7.cloned.1.call-update) | async-done | bytes 3145744 | tf_op jit(solution)/shard_map/all_gather | solution.py:85
  550.7 3.7 copy.217
  557.8 2.2 fusion.119
  570.0 2.4 concatenate.175.clone
  572.4 3.0 gather_fusion.33
  604.6 2.5 maximum_maximum_fusion.6
  607.1 6.4 maximum_maximum_fusion.2
  613.6 3.1 fusion.121
  638.8 3.3 maximum_maximum_fusion.3
  642.1 2.7 fusion.120
  687.0 12.2 %add_multiply_fusion = f32[1024,384]{1,0:T(8,128)S(1)} fusion(f32[1024,384]{1,0:T(8,128)} %fusion.12, f32[1024,384]{1,0:T(8,128)} %fusion.15, f32[1024,384]{1,0:T(8,128)} %fusion.18, f32[1024,384]{1,0:T(8,128)} %fusion.21, f32[1024,384]{1,0:T(8,128)} %fusion.24, f32[1024,384]{1,0:T(8,128)} %fusion.27, f32[1024,384]{1,0:T(8,128)} %fusion.30, ...), kind=kOutput, calls=%fused_computation.96 | convolution fusion | flops 312606720 | bytes 43552768 | tf_op jit(solution)/shard_map/dot_general | solution.py:98
  (487 shorter events, 245.7 us)
Async XLA Ops:
  7.2 44.0 %all-gather.5.cloned.1.call-start = ((), (), s32[]{:S(2)}) async-start(), calls=%async_computation.1 | async-start | bytes 3932160 | tf_op jit(solution)/shard_map/all_gather | solution.py:63
  7.9 239.1 %all-gather.9.cloned.1.call-start = ((), (), s32[]{:S(2)}) async-start(), calls=%async_computation.3 | async-start | bytes 8312832 | tf_op jit(solution)/shard_map/all_gather | solution.py:76
  8.6 516.5 %reduce-scatter.6.cloned.1.call-start = ((), (), s32[]{:S(2)}) async-start(), calls=%async_computation.4 | async-start | bytes 368640
  79.6 34.8 %copy-start.1 = (bf16[8,8,8,8,384]{4,3,2,1,0:T(8,128)(2,1)S(1)}, bf16[8,8,8,8,384]{4,3,2,1,0:T(8,128)(2,1)}, u32[]{:S(2)}) copy-start(bf16[8,8,8,8,384]{4,3,2,1,0:T(8,128)(2,1)} %copy.453) | copy-start | bytes 9437188
  82.4 9.3 %copy-start.4 = (bf16[9,8,8,384]{3,0,2,1:T(8,128)(2,1)S(1)}, bf16[9,8,8,384]{3,0,2,1:T(8,128)(2,1)}, u32[]{:S(2)}) copy-start(bf16[9,8,8,384]{3,0,2,1:T(8,128)(2,1)} %get-tuple-element.120) | copy-start | bytes 1327108
  116.8 28.2 %copy-start.60 = (bf16[2,8,384]{2,1,0:T(8,128)(2,1)S(1)}, bf16[2,8,384]{2,1,0:T(8,128)(2,1)}, u32[]{:S(2)}) copy-start(bf16[2,8,384]{2,1,0:T(8,128)(2,1)} %gather_fusion.17) | copy-start | bytes 36868
  116.8 28.2 %copy-start.65 = (pred[2]{0:T(512)(128)(4,1)S(1)}, pred[2]{0:T(512)(128)(4,1)}, u32[]{:S(2)}) copy-start(pred[2]{0:T(512)(128)(4,1)} %get-tuple-element.230) | copy-start | bytes 10
  116.8 28.3 %copy-start.61 = (bf16[2,8,384]{2,1,0:T(8,128)(2,1)S(1)}, bf16[2,8,384]{2,1,0:T(8,128)(2,1)}, u32[]{:S(2)}) copy-start(bf16[2,8,384]{2,1,0:T(8,128)(2,1)} %gather_fusion.19) | copy-start | bytes 36868
  116.8 28.3 %copy-start.63 = (pred[2]{0:T(512)(128)(4,1)S(1)}, pred[2]{0:T(512)(128)(4,1)}, u32[]{:S(2)}) copy-start(pred[2]{0:T(512)(128)(4,1)} %get-tuple-element.228) | copy-start | bytes 10
  116.8 28.4 %copy-start.66 = (pred[2]{0:T(512)(128)(4,1)S(1)}, pred[2]{0:T(512)(128)(4,1)}, u32[]{:S(2)}) copy-start(pred[2]{0:T(512)(128)(4,1)} %get-tuple-element.229) | copy-start | bytes 10
  116.8 28.5 %copy-start.67 = (pred[2]{0:T(512)(128)(4,1)S(1)}, pred[2]{0:T(512)(128)(4,1)}, u32[]{:S(2)}) copy-start(pred[2]{0:T(512)(128)(4,1)} %get-tuple-element.231) | copy-start | bytes 10
  116.8 28.7 %copy-start.69 = (pred[2]{0:T(512)(128)(4,1)S(1)}, pred[2]{0:T(512)(128)(4,1)}, u32[]{:S(2)}) copy-start(pred[2]{0:T(512)(128)(4,1)} %get-tuple-element.232) | copy-start | bytes 10
  246.9 9.3 %copy-start.50 = (bf16[1,2,512,384]{3,2,1,0:T(8,128)(2,1)S(1)}, bf16[1,2,512,384]{3,2,1,0:T(8,128)(2,1)}, u32[]{:S(2)}) copy-start(bf16[1,2,512,384]{3,2,1,0:T(8,128)(2,1)} %param.26) | copy-start | bytes 2359300
  274.5 18.0 %copy-start.49 = (bf16[1024,384]{1,0:T(8,128)(2,1)}, bf16[1024,384]{1,0:T(8,128)(2,1)S(1)}, u32[]{:S(2)}) copy-start(bf16[1024,384]{1,0:T(8,128)(2,1)S(1)} %fusion.3) | copy-start | bytes 2359300
  292.5 191.3 %copy-start.81 = (u32[128]{0:T(128)S(1)}, u32[128]{0:T(128)}, u32[]{:S(2)}) copy-start(u32[128]{0:T(128)} %constant.144) | copy-start | bytes 1540
  292.5 195.9 %copy-start.54 = (f32[324,96]{0,1:T(8,128)S(1)}, f32[324,96]{0,1:T(8,128)}, u32[]{:S(2)}) copy-start(f32[324,96]{0,1:T(8,128)} %param.30) | copy-start | bytes 373252
  479.6 8.9 %copy-start.55 = (f32[324,96]{0,1:T(8,128)S(1)}, f32[324,96]{0,1:T(8,128)}, u32[]{:S(2)}) copy-start(f32[324,96]{0,1:T(8,128)} %param.31) | copy-start | bytes 373252
  479.6 5.8 collective-permute-start
  481.1 3.9 collective-permute-start.1
  487.8 62.8 %all-gather.7.cloned.1.call-start = ((), (), s32[]{:S(2)}) async-start(), calls=%async_computation.2 | async-start | bytes 3932160 | tf_op jit(solution)/shard_map/all_gather | solution.py:85
  501.7 12.8 %copy-start = (bf16[384,27,384]{2,1,0:T(8,128)(2,1)S(1)}, bf16[384,27,384]{2,1,0:T(8,128)(2,1)}, u32[]{:S(2)}) copy-start(bf16[384,27,384]{2,1,0:T(8,128)(2,1)} %reshape.276) | copy-start | bytes 23887876
  562.1 7.2 %copy-start.68 = (pred[2]{0:T(512)(128)(4,1)S(1)}, pred[2]{0:T(512)(128)(4,1)}, u32[]{:S(2)}) copy-start(pred[2]{0:T(512)(128)(4,1)} %get-tuple-element.234) | copy-start | bytes 10
  572.4 8.0 %copy-start.22 = (bf16[9,8,8,384]{3,1,0,2:T(8,128)(2,1)S(1)}, bf16[9,8,8,384]{3,1,0,2:T(8,128)(2,1)}, u32[]{:S(2)}) copy-start(bf16[9,8,8,384]{3,1,0,2:T(8,128)(2,1)} %get-tuple-element.103) | copy-start | bytes 1327108
  572.4 9.6 %copy-start.21 = (bf16[9,8,8,384]{3,1,0,2:T(8,128)(2,1)S(1)}, bf16[9,8,8,384]{3,1,0,2:T(8,128)(2,1)}, u32[]{:S(2)}) copy-start(bf16[9,8,8,384]{3,1,0,2:T(8,128)(2,1)} %get-tuple-element.101) | copy-start | bytes 1327108
  576.2 14.1 %copy-start.53 = (bf16[9,1,1,8,384]{4,1,0,3,2:T(2,128)(2,1)S(1)}, bf16[9,1,1,8,384]{4,1,0,3,2:T(2,128)(2,1)}, u32[]{:S(2)}) copy-start(bf16[9,1,1,8,384]{4,1,0,3,2:T(2,128)(2,1)} %get-tuple-element.86) | copy-start | bytes 165892
  576.3 19.2 %copy-start.64 = (pred[2]{0:T(512)(128)(4,1)S(1)}, pred[2]{0:T(512)(128)(4,1)}, u32[]{:S(2)}) copy-start(pred[2]{0:T(512)(128)(4,1)} %get-tuple-element.228) | copy-start | bytes 10
  576.3 23.5 %copy-start.59 = (bf16[9,1,1,1,384]{4,1,0,3,2:T(2,128)(2,1)S(1)}, bf16[9,1,1,1,384]{4,1,0,3,2:T(2,128)(2,1)}, u32[]{:S(2)}) copy-start(bf16[9,1,1,1,384]{4,1,0,3,2:T(2,128)(2,1)} %get-tuple-element.85) | copy-start | bytes 20740
  576.3 24.9 %copy-start.58 = (bf16[9,1,1,1,384]{4,1,0,3,2:T(2,128)(2,1)S(1)}, bf16[9,1,1,1,384]{4,1,0,3,2:T(2,128)(2,1)}, u32[]{:S(2)}) copy-start(bf16[9,1,1,1,384]{4,1,0,3,2:T(2,128)(2,1)} %get-tuple-element.78) | copy-start | bytes 20740
  576.3 26.3 %copy-start.56 = (bf16[2,8,1,1,384]{4,3,1,0,2:T(2,128)(2,1)S(1)}, bf16[2,8,1,1,384]{4,3,1,0,2:T(2,128)(2,1)}, u32[]{:S(2)}) copy-start(bf16[2,8,1,1,384]{4,3,1,0,2:T(2,128)(2,1)} %copy.220) | copy-start | bytes 36868
  576.3 26.3 %copy-start.57 = (bf16[2,8,1,1,384]{4,3,1,0,2:T(2,128)(2,1)S(1)}, bf16[2,8,1,1,384]{4,3,1,0,2:T(2,128)(2,1)}, u32[]{:S(2)}) copy-start(bf16[2,8,1,1,384]{4,3,1,0,2:T(2,128)(2,1)} %broadcast_select_fusion.15) | copy-start | bytes 36868
  618.4 9.1 %copy-start.52 = (bf16[9,1,1,8,384]{4,1,0,3,2:T(2,128)(2,1)S(1)}, bf16[9,1,1,8,384]{4,1,0,3,2:T(2,128)(2,1)}, u32[]{:S(2)}) copy-start(bf16[9,1,1,8,384]{4,1,0,3,2:T(2,128)(2,1)} %get-tuple-element.87) | copy-start | bytes 165892
  687.0 12.2 %copy-start.51 = (bf16[1,2,512,384]{3,2,1,0:T(8,128)(2,1)S(1)}, bf16[1,2,512,384]{3,2,1,0:T(8,128)(2,1)}, u32[]{:S(2)}) copy-start(bf16[1,2,512,384]{3,2,1,0:T(8,128)(2,1)} %param.26) | copy-start | bytes 2359300
  (56 other events, 239.3 us)
Sparse Core Ops, SparseCore 0:
  9.7 41.5 all-gather.4
  54.3 103.0 all-gather.8
  488.0 21.7 reduce-scatter.5
  511.8 38.7 all-gather.6
where the time goes:
time: 716 us; the launch traced here: 707 us
  local copies, waits for them, and re-layouts  285 us (40%)
  blocking collectives  187 us (26%)
  matrix products  90.1 us (13%)
  other arithmetic  76.6 us (11%)
  waiting for transfers between devices  47.5 us (7%)
  between operations  16 us (2%)
    unnamed x1, blocking collectives  187 us
    gather x54, local copies, waits for them, and re-layouts, build_region(): pieces.append(jnp.take(window_part, neighbour_rows[:, offset_code], axis=0))  72.1 us
    dot_general x27, matrix products, body(): lax.dot_general(shifted(delta_region, 26 - offset), weight_cube[:, offset...  53.9 us
    unnamed x212, local copies, waits for them, and re-layouts  49.1 us
    another operation x2, local copies, waits for them, and re-layouts, column_block(): jnp.stack([shifted(region, offset) for offset in range(27)], axis=2)  32.3 us
    select_n x81, other arithmetic, build_region(): pieces.append(jnp.take(window_part, neighbour_rows[:, offset_code], axis=0))  28.3 us
    another operation x32, local copies, waits for them, and re-layouts, build_region(): pieces.append(jnp.take(window_part, neighbour_rows[:, offset_code], axis=0))  27.7 us
    reshape x1, local copies, waits for them, and re-layouts, column_block(): return stacked.reshape(stacked.shape[0], channel_count * 27)  26.7 us
  transfers between devices with their start and end apart: 6, of which 3 were waited for; matrix products, arithmetic and copies ran while one was open for 36% of the time, Pallas kernels for 0%

commit v1 on v0

v1 whole, which is shorter than its diff:
```python
import jax
import jax.numpy as jnp
from jax import lax
from jax.experimental import pallas as pl
from jax.experimental.pallas import tpu as pltpu
from jax.sharding import PartitionSpec as P

LIVE = 4
LANES = 128
CHUNK = 336
CUT = 176
MESH = pl.DeviceIdType.MESH
VMEM_BYTES = 58 * 1024 * 1024


def fill_regions(table, blocks, regions, live):
    channels = blocks.shape[-1]
    row = lax.broadcasted_iota(jnp.int32, (1, 8, channels), 1)

    def plane(step, carry):
        r = step // 10
        i = step % 10
        first = jnp.where(i == 0, 0, jnp.where(i == 9, 2, 1))
        source = (i + 7) % 8
        code = 9 * first
        for c in range(3):
            pieces = []
            for second, start, count in ((0, 7, 1), (1, 0, 8), (2, 0, 1)):
                where = pl.ds(source * 8 + start, count)
                values = blocks[table[r, code + 3 * second + 1], where]
                if c != 1:
                    edge = blocks[table[r, code + 3 * second + c], where]
                    values = jnp.where(row == (7 if c == 0 else 0), edge, values)
                    values = pltpu.roll(values, 1 if c == 0 else 7, 1)
                pieces.append(values)
            line = jnp.concatenate(pieces, axis=0)
            for b in range(3):
                regions[3 * b + c, r, i] = (
                    line[b : b + 8].reshape(64, channels).astype(jnp.bfloat16)
                )
        return carry

    lax.fori_loop(0, live * 10, plane, 0)


def shifted_rows(regions, block, k, channels):
    a, bc = k // 9, k % 9
    return regions[bc, block, a : a + 8].reshape(512, channels)


def forward_kernel(
    table, slots, feat, cot, parts, sums, delta, weight, blocks, regions, delta_t, stage
):
    live = slots.shape[0]
    channels = feat.shape[-1]
    for r in range(live):
        blocks[r] = feat[slots[r]].astype(jnp.float32).reshape(64, 8, channels)
    blocks[live] = jnp.zeros((64, 8, channels), jnp.float32)
    fill_regions(table, blocks, regions, live)

    rows_of = 27 * channels // 32
    for d in range(32):
        stage[rows_of * d : rows_of * d + CHUNK] = parts[d % 2, d // 8, d // 2 % 4].astype(
            jnp.float32
        )
    for k in range(27):
        weight[k * channels : (k + 1) * channels] = stage[
            pl.ds(k, channels, stride=27), :
        ].astype(jnp.bfloat16)

    def one_block(r, carry):
        pre = jnp.zeros((512, LANES), jnp.float32)
        for group in (range(g, min(g + 2, 27)) for g in range(0, 27, 2)):
            lhs = jnp.concatenate(
                [shifted_rows(regions, r, k, channels) for k in group], axis=1
            )
            rhs = weight[group[0] * channels : (group[-1] + 1) * channels]
            pre = pre + jnp.dot(lhs, rhs, preferred_element_type=jnp.float32)
        gate = jax.nn.sigmoid(pre)
        value = cot[slots[r]].astype(jnp.float32) * gate * (1.0 + pre * (1.0 - gate))
        delta[r] = value.astype(jnp.bfloat16)
        return carry

    lax.fori_loop(0, live, one_block, 0)
    for r in range(live):
        delta_t[:, r * 512 : (r + 1) * 512] = (
            delta[r].astype(jnp.float32).T.astype(jnp.bfloat16)
        )

    for k in range(27):
        rows = jnp.concatenate(
            [shifted_rows(regions, r, k, channels) for r in range(live)], axis=0
        )
        part = jnp.dot(delta_t[...], rows, preferred_element_type=jnp.float32)
        stage[pl.ds(k, channels, stride=27), :] = part.T
    for d in range(32):
        sums[d % 2, d // 8, d // 2 % 4] = stage[rows_of * d : rows_of * d + CHUNK].astype(
            jnp.bfloat16
        )


def backward_kernel(table, slots, delta, weight, back, blocks, regions):
    live = slots.shape[0]
    channels = back.shape[-1]
    for r in range(live):
        blocks[r] = delta[r].astype(jnp.float32).reshape(64, 8, LANES)
    blocks[live] = jnp.zeros((64, 8, LANES), jnp.float32)
    fill_regions(table, blocks, regions, live)
    back[...] = jnp.zeros(back.shape, back.dtype)

    def one_block(r, carry):
        total = jnp.zeros((512, channels), jnp.float32)
        for group in (range(g, min(g + 4, 27)) for g in range(0, 27, 4)):
            lhs = jnp.concatenate(
                [shifted_rows(regions, r, 26 - k, LANES) for k in group], axis=1
            )
            rhs = jnp.concatenate(
                [weight[k * channels : (k + 1) * channels] for k in group], axis=1
            )
            total = total + lax.dot_general(
                lhs, rhs, (((1,), (1,)), ((), ())), preferred_element_type=jnp.float32
            )
        back[slots[r]] = total.astype(jnp.bfloat16)
        return carry

    lax.fori_loop(0, live, one_block, 0)


SMEM_SPEC = pl.BlockSpec(memory_space=pltpu.SMEM)
VMEM_SPEC = pl.BlockSpec(memory_space=pltpu.VMEM)


def forward_call(table, slots, feat, cot, parts):
    live, channels = slots.shape[0], feat.shape[-1]
    flops = 2 * 2 * live * 512 * 27 * channels * LANES
    return pl.pallas_call(
        forward_kernel,
        out_shape=(
            jax.ShapeDtypeStruct((2, 4, 4, CHUNK, LANES), jnp.bfloat16),
            jax.ShapeDtypeStruct((live, 512, LANES), jnp.bfloat16),
            jax.ShapeDtypeStruct((27 * channels, LANES), jnp.bfloat16),
        ),
        in_specs=[SMEM_SPEC] * 2 + [VMEM_SPEC] * 3,
        out_specs=(VMEM_SPEC,) * 3,
        scratch_shapes=[
            pltpu.VMEM((live + 1, 64, 8, channels), jnp.float32),
            pltpu.VMEM((9, live, 10, 64, channels), jnp.bfloat16),
            pltpu.VMEM((LANES, live * 512), jnp.bfloat16),
            pltpu.VMEM((27 * channels + 16, LANES), jnp.float32),
        ],
        compiler_params=pltpu.CompilerParams(vmem_limit_bytes=VMEM_BYTES),
        cost_estimate=pl.CostEstimate(flops=flops, bytes_accessed=10**7, transcendentals=10**6),
    )(table, slots, feat, cot, parts)


class Wires:
    def __init__(self, send_sem, recv_sem):
        self.send_sem, self.recv_sem = send_sem, recv_sem
        dp, space = lax.axis_index("dp"), lax.axis_index("space")
        self.x, self.y, self.z = dp // 8, dp // 2 % 4, dp % 2
        self.chip, self.core = space // 2, space % 2
        self.started = []
        self.count = 0

    def at(self, x=None, y=None, z=None, chip=None, core=None):
        x, y, z = self.x if x is None else x, self.y if y is None else y, self.z if z is None else z
        chip, core = self.chip if chip is None else chip, self.core if core is None else core
        return (x * 8 + y * 2 + z, chip * 2 + core)

    def step(self, axis, by):
        return self.at(**{axis: (getattr(self, axis) + by) % 4})

    def meet(self, others):
        barrier = pltpu.get_barrier_semaphore()
        for other in others:
            pl.semaphore_signal(barrier, inc=1, device_id=other, device_id_type=MESH)
        pl.semaphore_wait(barrier, len(others))

    def everyone(self):
        return (
            [self.step(axis, by) for axis in ("x", "y") for by in (1, 3)]
            + [self.at(z=1 - self.z), self.at(chip=1 - self.chip), self.at(core=1 - self.core)]
            + [self.at(chip=1 - self.chip, core=1 - self.core)]
        )

    def ticket(self):
        self.count += 1
        return self.count - 1

    def send(self, ticket, source, target, other):
        copy = pltpu.make_async_remote_copy(
            source,
            target,
            self.send_sem.at[ticket],
            self.recv_sem.at[ticket],
            device_id=other,
            device_id_type=MESH,
        )
        copy.start()
        self.started.append(copy)

    def arrived(self, ticket, landing):
        pltpu.make_async_remote_copy(
            landing,
            landing,
            self.send_sem.at[ticket],
            self.recv_sem.at[ticket],
            device_id=self.at(core=1 - self.core),
            device_id_type=MESH,
        ).wait_recv()

    def finish(self):
        for copy in self.started:
            copy.wait_send()


class RingGather:
    def __init__(self, wires, axis, block):
        self.wires, self.axis, self.block = wires, axis, block
        self.q = getattr(wires, axis)
        self.tickets = [wires.ticket() for _ in range(6)]

    def start(self):
        t, q = self.tickets, self.q
        right, left = self.wires.step(self.axis, 1), self.wires.step(self.axis, 3)
        for ticket, half, other in ((t[0], 0, right), (t[1], 1, left), (t[2], 1, right), (t[3], 0, left)):
            mine = self.block(q, half)
            self.wires.send(ticket, mine, mine, other)

    def forward(self):
        t, q = self.tickets, self.q
        right, left = self.wires.step(self.axis, 1), self.wires.step(self.axis, 3)
        for ticket, into, half, source, other in (
            (t[0], t[4], 0, (q + 3) % 4, right),
            (t[1], t[5], 1, (q + 1) % 4, left),
        ):
            piece = self.block(source, half)
            self.wires.arrived(ticket, piece)
            self.wires.send(into, piece, piece, other)

    def end(self):
        t, q = self.tickets, self.q
        self.wires.arrived(t[2], self.block((q + 3) % 4, 1))
        self.wires.arrived(t[3], self.block((q + 1) % 4, 0))
        self.wires.arrived(t[4], self.block((q + 2) % 4, 0))
        self.wires.arrived(t[5], self.block((q + 2) % 4, 1))


def gather_kernel(rows, feat_own, cot_own, parts, feat, cot, local_sem, send_sem, recv_sem):
    w = Wires(send_sem, recv_sem)
    x, y, z = w.x, w.y, w.z
    me = w.chip * 2 + w.core
    over, beside = (1 - w.chip) * 2 + w.core, w.chip * 2 + 1 - w.core
    across = (1 - w.chip) * 2 + 1 - w.core
    to_over, to_beside = w.at(chip=1 - w.chip), w.at(core=1 - w.core)
    to_across = w.at(chip=1 - w.chip, core=1 - w.core)
    t_z, t_over, t_beside, t_across = (w.ticket() for _ in range(4))
    c_over, c_beside, c_across = (w.ticket() for _ in range(3))
    first_a = RingGather(w, "x", lambda q, h: parts.at[h, q, y, :CUT])
    first_b = RingGather(w, "y", lambda q, h: parts.at[h, x, q, CUT:])
    last_a = RingGather(w, "y", lambda q, h: parts.at[h, :, q, :CUT])
    last_b = RingGather(w, "x", lambda q, h: parts.at[h, q, :, CUT:])

    w.meet(w.everyone())
    w.send(t_z, rows, parts.at[z, x, y], w.at(z=1 - z))
    w.send(t_over, feat_own, feat.at[me], to_over)
    w.send(c_over, cot_own.at[over], cot.at[me], to_over)
    w.send(c_across, cot_own.at[across], cot.at[me], to_across)
    w.send(t_beside, feat_own, feat.at[me], to_beside)
    w.send(c_beside, cot_own.at[beside], cot.at[me], to_beside)
    keep = [
        pltpu.make_async_copy(rows, parts.at[z, x, y], local_sem.at[0]),
        pltpu.make_async_copy(feat_own, feat.at[me], local_sem.at[1]),
        pltpu.make_async_copy(cot_own.at[me], cot.at[me], local_sem.at[2]),
    ]
    for copy in keep:
        copy.start()
    keep[0].wait()
    w.arrived(t_z, parts.at[1 - z, x, y])
    first_a.start()
    first_b.start()
    first_a.forward()
    first_b.forward()
    first_a.end()
    first_b.end()
    last_a.start()
    last_b.start()
    last_a.forward()
    last_b.forward()
    w.arrived(t_over, feat.at[over])
    w.send(t_across, feat.at[over], feat.at[over], to_beside)
    last_a.end()
    last_b.end()
    w.arrived(t_beside, feat.at[beside])
    w.arrived(t_across, feat.at[across])
    w.arrived(c_over, cot.at[over])
    w.arrived(c_beside, cot.at[beside])
    w.arrived(c_across, cot.at[across])
    keep[1].wait()
    keep[2].wait()
    w.finish()


def gather_call(rows, feat_own, cot_own):
    spatial = cot_own.shape[0]
    copies = 7 + 4 * 6
    return pl.pallas_call(
        gather_kernel,
        out_shape=(
            jax.ShapeDtypeStruct((2, 4, 4) + rows.shape, rows.dtype),
            jax.ShapeDtypeStruct((spatial,) + feat_own.shape, feat_own.dtype),
            jax.ShapeDtypeStruct(cot_own.shape, cot_own.dtype),
        ),
        in_specs=[VMEM_SPEC] * 3,
        out_specs=(VMEM_SPEC,) * 3,
        scratch_shapes=[
            pltpu.SemaphoreType.DMA((3,)),
            pltpu.SemaphoreType.DMA((copies,)),
            pltpu.SemaphoreType.DMA((copies,)),
        ],
        compiler_params=pltpu.CompilerParams(
            collective_id=0, has_side_effects=True, vmem_limit_bytes=VMEM_BYTES
        ),
    )(rows, feat_own, cot_own)


class RingReduce:
    def __init__(self, wires, axis, block, near, far_left, far_right):
        self.wires, self.axis, self.block = wires, axis, block
        self.near, self.far = near, (far_left, far_right)
        self.q = getattr(wires, axis)
        self.tickets = [wires.ticket() for _ in range(6)]

    def start(self):
        w, t, q = self.wires, self.tickets, self.q
        right, left = w.step(self.axis, 1), w.step(self.axis, 3)
        w.send(t[0], self.block((q + 2) % 4, 0), self.near.at[0], right)
        w.send(t[1], self.block((q + 2) % 4, 1), self.near.at[1], left)
        w.send(t[2], self.block((q + 1) % 4, 1), self.far[0].at[1], right)
        w.send(t[3], self.block((q + 3) % 4, 0), self.far[1].at[0], left)

    def forward(self):
        w, t, q = self.wires, self.tickets, self.q
        right, left = w.step(self.axis, 1), w.step(self.axis, 3)
        for half, target, other in ((0, (q + 1) % 4, right), (1, (q + 3) % 4, left)):
            w.arrived(t[half], self.near.at[half])
            own = self.block(target, half)[...].astype(jnp.float32)
            self.near[half] = (self.near[half].astype(jnp.float32) + own).astype(jnp.bfloat16)
            w.send(t[4 + half], self.near.at[half], self.far[half].at[half], other)

    def end(self, out):
        w, t, q = self.wires, self.tickets, self.q
        w.arrived(t[2], self.far[0].at[1])
        w.arrived(t[3], self.far[1].at[0])
        w.arrived(t[4], self.far[0].at[0])
        w.arrived(t[5], self.far[1].at[1])
        for half in range(2):
            total = self.block(q, half)[...].astype(jnp.float32)
            total = total + self.far[0][half].astype(jnp.float32)
            total = total + self.far[1][half].astype(jnp.float32)
            out[half] = total.astype(out.dtype)


def reduce_kernel(
    sums, back, grad, total, a_near, a_left, a_right, b_near, b_left, b_right, a_mid, b_mid,
    c_near, c_left, c_right, d_near, d_left, d_right, last, from_z, from_core, to_chip, from_chip,
    send_sem, recv_sem,
):
    w = Wires(send_sem, recv_sem)
    x, y, z, chip, core = w.x, w.y, w.z, w.chip, w.core
    me, over, beside = chip * 2 + core, (1 - chip) * 2 + core, chip * 2 + 1 - core
    across = (1 - chip) * 2 + 1 - core
    to_over, to_beside = w.at(chip=1 - chip), w.at(core=1 - core)
    first_a = RingReduce(w, "y", lambda q, h: sums.at[h, :, q, :CUT], a_near, a_left, a_right)
    first_b = RingReduce(w, "x", lambda q, h: sums.at[h, q, :, CUT:], b_near, b_left, b_right)
    last_a = RingReduce(w, "x", lambda q, h: a_mid.at[h, q], c_near, c_left, c_right)
    last_b = RingReduce(w, "y", lambda q, h: b_mid.at[h, q], d_near, d_left, d_right)
    t_z, t_far, t_own, t_chip = (w.ticket() for _ in range(4))

    w.meet(w.everyone())
    first_a.start()
    first_b.start()
    w.send(t_far, back.at[across], from_core.at[1 - chip], to_beside)
    w.send(t_own, back.at[beside], from_core.at[chip], to_beside)
    w.arrived(t_far, from_core.at[1 - chip])
    to_chip[...] = (
        back[over].astype(jnp.float32) + from_core[1 - chip].astype(jnp.float32)
    ).astype(jnp.bfloat16)
    w.send(t_chip, to_chip, from_chip, to_over)
    first_a.forward()
    first_b.forward()
    w.arrived(t_own, from_core.at[chip])
    total[...] = back[me].astype(jnp.float32) + from_core[chip].astype(jnp.float32)
    first_a.end(a_mid)
    first_b.end(b_mid)
    last_a.start()
    last_b.start()
    last_a.forward()
    last_b.forward()
    last_a.end(last.at[:, :CUT])
    last_b.end(last.at[:, CUT:])
    w.send(t_z, last.at[1 - z], from_z, w.at(z=1 - z))
    w.arrived(t_chip, from_chip)
    total[...] = total[...] + from_chip[...].astype(jnp.float32)
    w.arrived(t_z, from_z)
    grad[...] = last[z].astype(jnp.float32) + from_z[...].astype(jnp.float32)
    w.finish()


def reduce_call(sums, back):
    spatial, capacity, voxels, channels = back.shape
    rest = CHUNK - CUT
    copies = 4 * 6 + 4

    def buffer(*shape):
        return pltpu.VMEM(shape + (LANES,), jnp.bfloat16)

    def ring(*shape):
        return [buffer(2, *shape)] * 3

    block = (capacity, voxels, channels)
    return pl.pallas_call(
        reduce_kernel,
        out_shape=(
            jax.ShapeDtypeStruct((CHUNK, LANES), jnp.float32),
            jax.ShapeDtypeStruct(block, jnp.float32),
        ),
        in_specs=[VMEM_SPEC] * 2,
        out_specs=(VMEM_SPEC,) * 2,
        scratch_shapes=ring(4, CUT)
        + ring(4, rest)
        + [buffer(2, 4, CUT), buffer(2, 4, rest)]
        + ring(CUT)
        + ring(rest)
        + [
            buffer(2, CHUNK),
            buffer(CHUNK),
            pltpu.VMEM((2,) + block, jnp.bfloat16),
            pltpu.VMEM(block, jnp.bfloat16),
            pltpu.VMEM(block, jnp.bfloat16),
            pltpu.SemaphoreType.DMA((copies,)),
            pltpu.SemaphoreType.DMA((copies,)),
        ],
        compiler_params=pltpu.CompilerParams(
            collective_id=1, has_side_effects=True, vmem_limit_bytes=VMEM_BYTES
        ),
    )(sums, back)


def backward_call(table, slots, delta, weight, capacity):
    live, channels = slots.shape[0], weight.shape[0] // 27
    flops = 2 * live * 512 * 27 * channels * LANES
    return pl.pallas_call(
        backward_kernel,
        out_shape=jax.ShapeDtypeStruct((capacity, 512, channels), jnp.bfloat16),
        in_specs=[SMEM_SPEC] * 2 + [VMEM_SPEC] * 2,
        out_specs=VMEM_SPEC,
        scratch_shapes=[
            pltpu.VMEM((live + 1, 64, 8, LANES), jnp.float32),
            pltpu.VMEM((9, live, 10, 64, LANES), jnp.bfloat16),
        ],
        compiler_params=pltpu.CompilerParams(vmem_limit_bytes=VMEM_BYTES),
        cost_estimate=pl.CostEstimate(flops=flops, bytes_accessed=10**7, transcendentals=0),
    )(table, slots, delta, weight)


def live_tables(links):
    group = links.shape[0]
    alive = links[:, 13] >= 0
    order = jnp.arange(group, dtype=jnp.int32)
    before = (order[None, :] < order[:, None]) & alive[None, :]
    rank = jnp.sum(before.astype(jnp.int32), axis=1)
    places = jnp.arange(LIVE, dtype=jnp.int32)
    chosen = ((rank[None, :] == places[:, None]) & alive[None, :]).astype(jnp.int32)
    slots = jnp.sum(chosen * jnp.arange(group, dtype=jnp.int32)[None, :], axis=1)
    rows = jnp.sum(chosen[:, :, None] * links[None, :, :], axis=1)
    named = (rows[:, :, None] == jnp.arange(group, dtype=jnp.int32)).astype(jnp.int32)
    table = jnp.sum(named * (rank - LIVE)[None, None, :], axis=2) + LIVE
    return table.astype(jnp.int32), slots.astype(jnp.int32)


def body(features, cotangent, weight, occupancy, neighbours, first_moment, second_moment):
    channels = features.shape[3]
    capacity = features.shape[1]
    spatial = lax.axis_size("space")
    position = lax.axis_index("space")
    width = channels // spatial
    pad = ((0, 0), (0, 0), (0, LANES - width))
    table, slots = live_tables(neighbours[0])
    own = lax.dynamic_slice_in_dim(occupancy[0], position * capacity, capacity, 0)
    mask = own.astype(jnp.bfloat16)[:, :, None]

    narrow = lax.dynamic_slice_in_dim(weight, position * width, width, 1)
    narrow = jnp.pad(narrow, ((0, CHUNK - narrow.shape[0]), (0, LANES - width)))
    cot = (cotangent[0] * mask).reshape(capacity, 512, spatial, width)
    cot = jnp.pad(cot.transpose(2, 0, 1, 3), ((0, 0),) + pad)
    parts, feat, cot = gather_call(narrow, features[0] * mask, cot)
    feat = feat.reshape(spatial * capacity, 512, channels)
    cot = cot.reshape(spatial * capacity, 512, LANES)

    sums, delta, kernel = forward_call(table, slots, feat, cot, parts)
    back = backward_call(table, slots, delta, kernel, spatial * capacity)
    summed, back = reduce_call(sums, back.reshape(spatial, capacity, 512, channels))
    summed = summed[: weight.shape[0], :width]
    back = back * own.astype(jnp.float32)[:, :, None]
    input_grad = (cotangent[0].astype(jnp.float32) + back).astype(jnp.bfloat16)[None]

    scaled = summed / 64.0
    new_first = 0.9 * first_moment + 0.1 * scaled
    new_second = 0.999 * second_moment + 0.001 * scaled * scaled
    return input_grad, new_first, new_second


def solution(mesh):
    return jax.shard_map(
        body,
        mesh=mesh,
        in_specs=(
            P("dp", "space", None, None),
            P("dp", "space", None, None),
            P("dp", None),
            P("dp", None, None),
            P("dp", None, None),
            P("dp", "space"),
            P("dp", "space"),
        ),
        out_specs=(P("dp", "space", None, None), P("dp", "space"), P("dp", "space")),
        check_vma=False,
    )
```

time: 716 us -> 131 us (0.18); the launches traced: 707 us -> 129 us
  local copies, waits for them, and re-layouts: 285 us -> 5.9 us
  blocking collectives: 187 us -> 0 us
  Pallas kernels: 0 us -> 115 us
  matrix products: 90.1 us -> 0 us
  other arithmetic: 76.6 us -> 7.31 us
  waiting for transfers between devices: 47.5 us -> 0 us
  between operations: 16 us -> 0.76 us
    unnamed x1 -> x0, blocking collectives: 187 us -> none
    pallas_call x0 -> x4, Pallas kernels: none -> 115 us  [the longest x1 41 us: gather_call(): pl.pallas_call(gather_kernel, out_shape=(jax.ShapeDtypeStruct((2, 4, 4) +...]
    dot_general x29 -> x0, matrix products: 90.1 us -> none  [the longest x27 53.9 us: body(): lax.dot_general(shifted(delta_region, 26 - offset), weight_cube[:, offset...]
    gather x56 -> x0, local copies, waits for them, and re-layouts: 73.2 us -> none  [the longest x54 72.1 us: build_region(): pieces.append(jnp.take(window_part, neighbour_rows[:, offset_code], axis=0))]
    another operation x34 -> x0, local copies, waits for them, and re-layouts: 60 us -> none  [the longest x2 32.3 us: column_block(): jnp.stack([shifted(region, offset) for offset in range(27)], axis=2)]
    slice x26 -> x0, local copies, waits for them, and re-layouts: 48.2 us -> none  [the longest x2 23.4 us: body(): weight_cube[:, offset, :]]
    unnamed x212 -> x17, local copies, waits for them, and re-layouts: 49.1 us -> 3.22 us
    all_gather x3 -> x0, waiting for transfers between devices: 45.1 us -> none  [the longest x1 22.8 us: body(): delta_all = lax.all_gather(delta_blocks, 'space', axis=0, tiled=True)]
  transfers between devices with their start and end apart: 6 -> 0, of which waited for: 3 -> 0; matrix products, arithmetic and copies ran while one was open for 36% -> 0% of each run, Pallas kernels for 0% -> 0%
where the time goes in v1:
time: 131 us; the launch traced here: 129 us
  Pallas kernels  115 us (88%)
  other arithmetic  7.31 us (6%)
  local copies, waits for them, and re-layouts  5.9 us (5%)
    pallas_call x1, Pallas kernels, gather_call(): pl.pallas_call(gather_kernel, out_shape=(jax.ShapeDtypeStruct((2, 4, 4) +...  41 us
    pallas_call x1, Pallas kernels, reduce_call(): pl.pallas_call(reduce_kernel, out_shape=(jax.ShapeDtypeStruct((CHUNK, LAN...  31.7 us
    pallas_call x1, Pallas kernels, forward_call(): pl.pallas_call(forward_kernel, out_shape=(jax.ShapeDtypeStruct((2, 4, 4,...  28.5 us
    pallas_call x1, Pallas kernels, backward_call(): pl.pallas_call(backward_kernel, out_shape=jax.ShapeDtypeStruct((capacity,...  14.2 us
    unnamed x17, local copies, waits for them, and re-layouts  3.22 us

profile of v1, /device:TPU:1, one launch (start us, length us, event | category | flops | bytes accessed | tf_op | source)
XLA Modules:
  0.0 129.5 jit_solution(3837117842565266530)
XLA Ops:
  0.6 0.0 copy-start
  0.7 0.8 convert_bitcast_fusion
  1.4 1.4 %copy.20 = bf16[1,2,512,384]{2,3,1,0:T(8,128)(2,1)S(1)} copy(bf16[1,2,512,384]{3,2,1,0:T(8,128)(2,1)} %param.8) | data formatting | bytes 1572864 | tf_op args[1]
  2.8 0.7 copy.21
  3.5 0.2 multiply_bitcast_fusion
  3.7 0.0 copy-start.2
  3.7 1.3 pad.9.cot_own
  5.0 0.0 copy-done.2
  5.0 1.1 bitcast_multiply_fusion.feat_own
  6.1 0.0 copy-done
  6.1 0.1 constant_dynamic-slice_fusion
  6.2 0.7 pad.8.rows
  6.8 41.0 %shard_map.94 = (bf16[2,4,4,336,128]{4,3,2,1,0:T(8,128)(2,1)}, bf16[4,2,512,384]{3,2,1,0:T(8,128)(2,1)}, bf16[4,2,512,128]{3,2,1,0:T(8,128)(2,1)}) custom-call(bf16[336,128]{1,0:T(8,128)(2,1)} %pad.8.rows, bf16[2,512,384]{2,1,0:T(8,128)(2,1)} %bitcast_multiply_fusion.feat_own, bf16[4,2,512,128]{3,2,1,0:T(8,128)(2,1)} %pad.9.cot_own), custom_call_target="tpu_custom_call" | custom-call | tf_op jit(solution)/shard_map/pallas_call | solution.py:307
  47.9 0.0 copy-done.5
  47.9 0.2 fusion.3
  48.1 0.1 convert_reduce_fusion
  48.2 0.1 multiply_reduce_fusion
  48.3 0.1 select_reduce_fusion
  48.4 0.6 broadcast_add_fusion.table
  49.0 0.6 select_reduce_fusion.1.slots
  49.6 28.5 %shard_map.95 = (bf16[2,4,4,336,128]{4,3,2,1,0:T(8,128)(2,1)}, bf16[4,512,128]{2,1,0:T(8,128)(2,1)}, bf16[10368,128]{1,0:T(8,128)(2,1)}) custom-call(s32[4,27]{1,0:T(4,128)} %broadcast_add_fusion.table, s32[4]{0:T(128)} %select_reduce_fusion.1.slots, bf16[8,512,384]{2,1,0:T(8,128)(2,1)} %bitcast.22, bf16[8,512,128]{2,1,0:T(8,128)(2,1)} %bitcast.23, ...), custom_call_target="tpu_custom_call" | custom-call | flops 10871635968 | bytes 10000000 | tf_op jit(solution)/shard_map/pallas_call | solution.py:136
  78.1 14.2 %shard_map.96 = bf16[8,512,384]{2,1,0:T(8,128)(2,1)} custom-call(s32[4,27]{1,0:T(4,128)} %broadcast_add_fusion.table, s32[4]{0:T(128)} %select_reduce_fusion.1.slots, bf16[4,512,128]{2,1,0:T(8,128)(2,1)} %get-tuple-element.15.delta, bf16[10368,128]{1,0:T(8,128)(2,1)} %get-tuple-element.16.weight), custom_call_target="tpu_custom_call" | custom-call | flops 5435817984 | bytes 10000000 | tf_op jit(solution)/shard_map/pallas_call | solution.py:453
  92.3 31.7 %shard_map.97 = (f32[336,128]{1,0:T(8,128)}, f32[2,512,384]{2,1,0:T(8,128)}) custom-call(bf16[2,4,4,336,128]{4,3,2,1,0:T(8,128)(2,1)} %get-tuple-element.14.sums, bf16[4,2,512,384]{3,2,1,0:T(8,128)(2,1)} %bitcast.19), custom_call_target="tpu_custom_call" | custom-call | tf_op jit(solution)/shard_map/pallas_call | solution.py:422
  124.1 0.0 copy-start.1
  124.1 0.0 copy-done.3
  124.1 0.1 copy.22
  124.2 0.0 copy-done.4
  124.2 0.1 copy.23
  124.3 1.0 multiply_add_fusion
  125.3 0.8 copy.24
  126.1 0.8 copy.25
  126.9 2.6 %fusion.1 = bf16[1,2,512,384]{3,2,1,0:T(8,128)(2,1)} fusion(f32[2,512,384]{2,1,0:T(8,128)} %get-tuple-element.17, bf16[1,2,512,384]{3,2,1,0:T(8,128)(2,1)S(1)} %copy-done.1, f32[2,512]{1,0:T(2,128)S(1)} %get-tuple-element.30), kind=kLoop, calls=%fused_computation.3 | loop fusion | flops 1572864 | bytes 3149824 | tf_op jit(solution)/shard_map/broadcast_in_dim | solution.py:506
  (6 shorter events, 0.0 us)
Async XLA Ops:
  0.6 5.5 %copy-start = (bf16[324,384]{1,0:T(8,128)(2,1)S(1)}, bf16[324,384]{1,0:T(8,128)(2,1)}, u32[]{:S(2)}) copy-start(bf16[324,384]{1,0:T(8,128)(2,1)} %param.9) | copy-start | bytes 746500
  3.7 1.3 copy-start.2
  5.0 42.9 %copy-start.5 = (s32[1,8,27]{2,1,0:T(8,128)S(1)}, s32[1,8,27]{2,1,0:T(8,128)}, u32[]{:S(2)}) copy-start(s32[1,8,27]{2,1,0:T(8,128)} %param.11) | copy-start | bytes 2596
  92.3 31.8 %copy-start.3 = (f32[324,96]{0,1:T(8,128)S(1)}, f32[324,96]{0,1:T(8,128)}, u32[]{:S(2)}) copy-start(f32[324,96]{0,1:T(8,128)} %param.12) | copy-start | bytes 373252
  92.3 31.9 %copy-start.4 = (f32[324,96]{0,1:T(8,128)S(1)}, f32[324,96]{0,1:T(8,128)}, u32[]{:S(2)}) copy-start(f32[324,96]{0,1:T(8,128)} %param.13) | copy-start | bytes 373252
  124.1 2.8 %copy-start.1 = (bf16[1,2,512,384]{3,2,1,0:T(8,128)(2,1)S(1)}, bf16[1,2,512,384]{3,2,1,0:T(8,128)(2,1)}, u32[]{:S(2)}) copy-start(bf16[1,2,512,384]{3,2,1,0:T(8,128)(2,1)} %param.8) | copy-start | bytes 2359300

commit v2 on v1

v2 whole, which is shorter than its diff:
```python
import jax
import jax.numpy as jnp
from jax import lax
from jax.experimental import pallas as pl
from jax.experimental.pallas import tpu as pltpu
from jax.sharding import PartitionSpec as P

LIVE = 4
LANES = 128
CHUNK = 336
CUT = 176
MESH = pl.DeviceIdType.MESH
VMEM_BYTES = 62 * 1024 * 1024


def fill_regions(table, blocks, regions, live):
    channels = blocks.shape[-1]
    row = lax.broadcasted_iota(jnp.int32, (1, 8, channels), 1)

    def plane(step, carry):
        r = step // 10
        i = step % 10
        first = jnp.where(i == 0, 0, jnp.where(i == 9, 2, 1))
        source = (i + 7) % 8
        code = 9 * first
        for c in range(3):
            pieces = []
            for second, start, count in ((0, 7, 1), (1, 0, 8), (2, 0, 1)):
                where = pl.ds(source * 8 + start, count)
                values = blocks[table[r, code + 3 * second + 1], where]
                if c != 1:
                    edge = blocks[table[r, code + 3 * second + c], where]
                    values = jnp.where(row == (7 if c == 0 else 0), edge, values)
                    values = pltpu.roll(values, 1 if c == 0 else 7, 1)
                pieces.append(values)
            line = jnp.concatenate(pieces, axis=0)
            for b in range(3):
                regions[3 * b + c, r, i] = (
                    line[b : b + 8].reshape(64, channels).astype(jnp.bfloat16)
                )
        return carry

    lax.fori_loop(0, live * 10, plane, 0)


def shifted_rows(regions, block, k, channels):
    a, bc = k // 9, k % 9
    return regions[bc, block, a : a + 8].reshape(512, channels)


SMEM_SPEC = pl.BlockSpec(memory_space=pltpu.SMEM)
VMEM_SPEC = pl.BlockSpec(memory_space=pltpu.VMEM)


class Wires:
    def __init__(self, send_sem, recv_sem):
        self.send_sem, self.recv_sem = send_sem, recv_sem
        dp, space = lax.axis_index("dp"), lax.axis_index("space")
        self.x, self.y, self.z = dp // 8, dp // 2 % 4, dp % 2
        self.chip, self.core = space // 2, space % 2
        self.started = []
        self.count = 0

    def at(self, x=None, y=None, z=None, chip=None, core=None):
        x, y, z = self.x if x is None else x, self.y if y is None else y, self.z if z is None else z
        chip, core = self.chip if chip is None else chip, self.core if core is None else core
        return (x * 8 + y * 2 + z, chip * 2 + core)

    def step(self, axis, by):
        return self.at(**{axis: (getattr(self, axis) + by) % 4})

    def meet(self, others):
        barrier = pltpu.get_barrier_semaphore()
        for other in others:
            pl.semaphore_signal(barrier, inc=1, device_id=other, device_id_type=MESH)
        pl.semaphore_wait(barrier, len(others))

    def everyone(self):
        return (
            [self.step(axis, by) for axis in ("x", "y") for by in (1, 3)]
            + [self.at(z=1 - self.z), self.at(chip=1 - self.chip), self.at(core=1 - self.core)]
            + [self.at(chip=1 - self.chip, core=1 - self.core)]
        )

    def ticket(self):
        self.count += 1
        return self.count - 1

    def send(self, ticket, source, target, other):
        copy = pltpu.make_async_remote_copy(
            source,
            target,
            self.send_sem.at[ticket],
            self.recv_sem.at[ticket],
            device_id=other,
            device_id_type=MESH,
        )
        copy.start()
        self.started.append(copy)

    def arrived(self, ticket, landing):
        pltpu.make_async_remote_copy(
            landing,
            landing,
            self.send_sem.at[ticket],
            self.recv_sem.at[ticket],
            device_id=self.at(core=1 - self.core),
            device_id_type=MESH,
        ).wait_recv()

    def finish(self):
        for copy in self.started:
            copy.wait_send()
        self.started = []


class RingGather:
    def __init__(self, wires, axis, block):
        self.wires, self.axis, self.block = wires, axis, block
        self.q = getattr(wires, axis)
        self.tickets = [wires.ticket() for _ in range(6)]

    def start(self):
        t, q = self.tickets, self.q
        right, left = self.wires.step(self.axis, 1), self.wires.step(self.axis, 3)
        for ticket, half, other in ((t[0], 0, right), (t[1], 1, left), (t[2], 1, right), (t[3], 0, left)):
            mine = self.block(q, half)
            self.wires.send(ticket, mine, mine, other)

    def forward(self):
        t, q = self.tickets, self.q
        right, left = self.wires.step(self.axis, 1), self.wires.step(self.axis, 3)
        for ticket, into, half, source, other in (
            (t[0], t[4], 0, (q + 3) % 4, right),
            (t[1], t[5], 1, (q + 1) % 4, left),
        ):
            piece = self.block(source, half)
            self.wires.arrived(ticket, piece)
            self.wires.send(into, piece, piece, other)

    def end(self):
        t, q = self.tickets, self.q
        self.wires.arrived(t[2], self.block((q + 3) % 4, 1))
        self.wires.arrived(t[3], self.block((q + 1) % 4, 0))
        self.wires.arrived(t[4], self.block((q + 2) % 4, 0))
        self.wires.arrived(t[5], self.block((q + 2) % 4, 1))


class RingReduce:
    def __init__(self, wires, axis, block, near, far_left, far_right):
        self.wires, self.axis, self.block = wires, axis, block
        self.near, self.far = near, (far_left, far_right)
        self.q = getattr(wires, axis)
        self.tickets = [wires.ticket() for _ in range(6)]

    def start(self):
        w, t, q = self.wires, self.tickets, self.q
        right, left = w.step(self.axis, 1), w.step(self.axis, 3)
        w.send(t[0], self.block((q + 2) % 4, 0), self.near.at[0], right)
        w.send(t[1], self.block((q + 2) % 4, 1), self.near.at[1], left)
        w.send(t[2], self.block((q + 1) % 4, 1), self.far[0].at[1], right)
        w.send(t[3], self.block((q + 3) % 4, 0), self.far[1].at[0], left)

    def forward(self):
        w, t, q = self.wires, self.tickets, self.q
        right, left = w.step(self.axis, 1), w.step(self.axis, 3)
        for half, target, other in ((0, (q + 1) % 4, right), (1, (q + 3) % 4, left)):
            w.arrived(t[half], self.near.at[half])
            own = self.block(target, half)[...].astype(jnp.float32)
            self.near[half] = (self.near[half].astype(jnp.float32) + own).astype(jnp.bfloat16)
            w.send(t[4 + half], self.near.at[half], self.far[half].at[half], other)

    def end(self, out):
        w, t, q = self.wires, self.tickets, self.q
        w.arrived(t[2], self.far[0].at[1])
        w.arrived(t[3], self.far[1].at[0])
        w.arrived(t[4], self.far[0].at[0])
        w.arrived(t[5], self.far[1].at[1])
        for half in range(2):
            total = self.block(q, half)[...].astype(jnp.float32)
            total = total + self.far[0][half].astype(jnp.float32)
            total = total + self.far[1][half].astype(jnp.float32)
            out[half] = total.astype(out.dtype)


def step_kernel(
    table, slots, places, rows, feat_own, cot_own, grad, total,
    parts, feat, cot, blocks, regions, delta, delta_t, stage, weight, thin, back_live, back,
    a_near, a_left, a_right, b_near, b_left, b_right, a_mid, b_mid,
    c_near, c_left, c_right, d_near, d_left, d_right, last, from_z, from_core, to_chip, from_chip,
    local_sem, send_sem, recv_sem,
):
    live, group = slots.shape[0], places.shape[0]
    capacity, channels = feat_own.shape[0], feat_own.shape[2]
    rows_of = 27 * channels // 32
    w = Wires(send_sem, recv_sem)
    x, y, z, chip, core = w.x, w.y, w.z, w.chip, w.core
    me, over, beside = chip * 2 + core, (1 - chip) * 2 + core, chip * 2 + 1 - core
    across = (1 - chip) * 2 + 1 - core
    to_over, to_beside = w.at(chip=1 - chip), w.at(core=1 - core)
    to_across = w.at(chip=1 - chip, core=1 - core)
    t_z, t_over, t_beside, t_across = (w.ticket() for _ in range(4))
    c_over, c_beside, c_across = (w.ticket() for _ in range(3))
    first_a = RingGather(w, "x", lambda q, h: parts.at[h, q, y, :CUT])
    first_b = RingGather(w, "y", lambda q, h: parts.at[h, x, q, CUT:])
    last_a = RingGather(w, "y", lambda q, h: parts.at[h, :, q, :CUT])
    last_b = RingGather(w, "x", lambda q, h: parts.at[h, q, :, CUT:])
    sum_a = RingReduce(w, "y", lambda q, h: parts.at[h, :, q, :CUT], a_near, a_left, a_right)
    sum_b = RingReduce(w, "x", lambda q, h: parts.at[h, q, :, CUT:], b_near, b_left, b_right)
    end_a = RingReduce(w, "x", lambda q, h: a_mid.at[h, q], c_near, c_left, c_right)
    end_b = RingReduce(w, "y", lambda q, h: b_mid.at[h, q], d_near, d_left, d_right)
    t_out, t_far, t_own, t_chip = (w.ticket() for _ in range(4))

    w.meet(w.everyone())
    w.send(t_z, rows, parts.at[z, x, y], w.at(z=1 - z))
    w.send(t_over, feat_own, feat.at[me], to_over)
    w.send(t_beside, feat_own, feat.at[me], to_beside)
    w.send(c_beside, cot_own.at[beside], cot.at[me], to_beside)
    keep = [
        pltpu.make_async_copy(rows, parts.at[z, x, y], local_sem.at[0]),
        pltpu.make_async_copy(feat_own, feat.at[me], local_sem.at[1]),
        pltpu.make_async_copy(cot_own.at[me], cot.at[me], local_sem.at[2]),
    ]
    for copy in keep:
        copy.start()
    keep[0].wait()
    w.arrived(t_z, parts.at[1 - z, x, y])
    first_a.start()
    first_b.start()
    first_a.forward()
    first_b.forward()
    first_a.end()
    first_b.end()
    last_a.start()
    last_b.start()
    w.arrived(t_over, feat.at[over])
    w.send(t_across, feat.at[over], feat.at[over], to_beside)
    w.send(c_over, cot_own.at[over], cot.at[me], to_over)
    w.send(c_across, cot_own.at[across], cot.at[me], to_across)
    last_a.forward()
    last_b.forward()
    keep[1].wait()
    keep[2].wait()
    w.arrived(t_beside, feat.at[beside])
    w.arrived(t_across, feat.at[across])

    for r in range(live):
        blocks[r] = feat[slots[r] // capacity, slots[r] % capacity].astype(jnp.float32).reshape(
            64, 8, channels
        )
    blocks[live] = jnp.zeros((64, 8, channels), jnp.float32)
    fill_regions(table, blocks, regions, live)
    last_a.end()
    last_b.end()
    for d in range(32):
        stage[rows_of * d : rows_of * d + CHUNK] = parts[d % 2, d // 8, d // 2 % 4].astype(
            jnp.float32
        )
    for k in range(27):
        weight[k * channels : (k + 1) * channels] = stage[
            pl.ds(k, channels, stride=27), :
        ].astype(jnp.bfloat16)
    w.arrived(c_over, cot.at[over])
    w.arrived(c_beside, cot.at[beside])
    w.arrived(c_across, cot.at[across])

    def forward_block(r, carry):
        pre = jnp.zeros((512, LANES), jnp.float32)
        for ks in (range(g, min(g + 2, 27)) for g in range(0, 27, 2)):
            lhs = jnp.concatenate([shifted_rows(regions, r, k, channels) for k in ks], axis=1)
            rhs = weight[ks[0] * channels : (ks[-1] + 1) * channels]
            pre = pre + jnp.dot(lhs, rhs, preferred_element_type=jnp.float32)
        gate = jax.nn.sigmoid(pre)
        value = cot[slots[r] // capacity, slots[r] % capacity].astype(jnp.float32)
        delta[r] = (value * gate * (1.0 + pre * (1.0 - gate))).astype(jnp.bfloat16)
        return carry

    lax.fori_loop(0, live, forward_block, 0)
    for r in range(live):
        delta_t[:, r * 512 : (r + 1) * 512] = (
            delta[r].astype(jnp.float32).T.astype(jnp.bfloat16)
        )
    for k in range(27):
        field = jnp.concatenate(
            [shifted_rows(regions, r, k, channels) for r in range(live)], axis=0
        )
        part = jnp.dot(delta_t[...], field, preferred_element_type=jnp.float32)
        stage[pl.ds(k, channels, stride=27), :] = part.T
    w.finish()
    for d in range(32):
        parts[d % 2, d // 8, d // 2 % 4] = stage[rows_of * d : rows_of * d + CHUNK].astype(
            jnp.bfloat16
        )
    sum_a.start()
    sum_b.start()

    for r in range(live):
        thin[r] = delta[r].astype(jnp.float32).reshape(64, 8, LANES)
    thin[live] = jnp.zeros((64, 8, LANES), jnp.float32)
    narrow = regions.at[:, :, :, :, :LANES]
    fill_regions(table, thin, narrow, live)
    back_live[live] = jnp.zeros((512, channels), jnp.bfloat16)

    def back_block(r, carry):
        out = jnp.zeros((512, channels), jnp.float32)
        for ks in (range(g, min(g + 4, 27)) for g in range(0, 27, 4)):
            lhs = jnp.concatenate([shifted_rows(narrow, r, 26 - k, LANES) for k in ks], axis=1)
            rhs = jnp.concatenate(
                [weight[k * channels : (k + 1) * channels] for k in ks], axis=1
            )
            out = out + lax.dot_general(
                lhs, rhs, (((1,), (1,)), ((), ())), preferred_element_type=jnp.float32
            )
        back_live[r] = out.astype(jnp.bfloat16)
        return carry

    lax.fori_loop(0, live // 2, back_block, 0)
    sum_a.forward()
    sum_b.forward()
    lax.fori_loop(live // 2, live, back_block, 0)
    for slot in range(group):
        back[slot // capacity, slot % capacity] = back_live[places[slot]]
    w.send(t_far, back.at[across], from_core.at[1 - chip], to_beside)
    w.send(t_own, back.at[beside], from_core.at[chip], to_beside)
    sum_a.end(a_mid)
    sum_b.end(b_mid)
    end_a.start()
    end_b.start()
    w.arrived(t_far, from_core.at[1 - chip])
    to_chip[...] = (
        back[over].astype(jnp.float32) + from_core[1 - chip].astype(jnp.float32)
    ).astype(jnp.bfloat16)
    w.send(t_chip, to_chip, from_chip, to_over)
    end_a.forward()
    end_b.forward()
    w.arrived(t_own, from_core.at[chip])
    total[...] = back[me].astype(jnp.float32) + from_core[chip].astype(jnp.float32)
    end_a.end(last.at[:, :CUT])
    end_b.end(last.at[:, CUT:])
    w.send(t_out, last.at[1 - z], from_z, w.at(z=1 - z))
    w.arrived(t_out, from_z)
    grad[...] = last[z].astype(jnp.float32) + from_z[...].astype(jnp.float32)
    w.arrived(t_chip, from_chip)
    total[...] = total[...] + from_chip[...].astype(jnp.float32)
    w.finish()


def step_call(table, slots, places, rows, feat_own, cot_own):
    live, spatial = slots.shape[0], cot_own.shape[0]
    channels = feat_own.shape[2]
    rest = CHUNK - CUT
    copies = 8 * 6 + 11

    def buffer(*shape):
        return pltpu.VMEM(shape, jnp.bfloat16)

    def wide(*shape):
        return pltpu.VMEM(shape, jnp.float32)

    def ring(*shape):
        return [buffer(2, *shape, LANES)] * 3

    block = feat_own.shape
    flops = 3 * 2 * live * 512 * 27 * channels * LANES
    return pl.pallas_call(
        step_kernel,
        out_shape=(
            jax.ShapeDtypeStruct((CHUNK, LANES), jnp.float32),
            jax.ShapeDtypeStruct(block, jnp.float32),
        ),
        in_specs=[SMEM_SPEC] * 3 + [VMEM_SPEC] * 3,
        out_specs=(VMEM_SPEC,) * 2,
        scratch_shapes=[
            buffer(2, 4, 4, CHUNK, LANES),
            buffer(spatial, *block),
            buffer(*cot_own.shape),
            wide(live + 1, 64, 8, channels),
            buffer(9, live, 10, 64, channels),
            buffer(live, 512, LANES),
            buffer(LANES, live * 512),
            wide(27 * channels + 16, LANES),
            buffer(27 * channels, LANES),
            wide(live + 1, 64, 8, LANES),
            buffer(live + 1, 512, channels),
            buffer(spatial, *block),
        ]
        + ring(4, CUT)
        + ring(4, rest)
        + [buffer(2, 4, CUT, LANES), buffer(2, 4, rest, LANES)]
        + ring(CUT)
        + ring(rest)
        + [
            buffer(2, CHUNK, LANES),
            buffer(CHUNK, LANES),
            buffer(2, *block),
            buffer(*block),
            buffer(*block),
            pltpu.SemaphoreType.DMA((3,)),
            pltpu.SemaphoreType.DMA((copies,)),
            pltpu.SemaphoreType.DMA((copies,)),
        ],
        compiler_params=pltpu.CompilerParams(
            collective_id=0, has_side_effects=True, vmem_limit_bytes=VMEM_BYTES
        ),
        cost_estimate=pl.CostEstimate(flops=flops, bytes_accessed=10**7, transcendentals=10**6),
    )(table, slots, places, rows, feat_own, cot_own)


def live_tables(links):
    group = links.shape[0]
    alive = links[:, 13] >= 0
    order = jnp.arange(group, dtype=jnp.int32)
    before = (order[None, :] < order[:, None]) & alive[None, :]
    rank = jnp.sum(before.astype(jnp.int32), axis=1)
    places = jnp.arange(LIVE, dtype=jnp.int32)
    chosen = ((rank[None, :] == places[:, None]) & alive[None, :]).astype(jnp.int32)
    slots = jnp.sum(chosen * jnp.arange(group, dtype=jnp.int32)[None, :], axis=1)
    rows = jnp.sum(chosen[:, :, None] * links[None, :, :], axis=1)
    named = (rows[:, :, None] == jnp.arange(group, dtype=jnp.int32)).astype(jnp.int32)
    table = jnp.sum(named * (rank - LIVE)[None, None, :], axis=2) + LIVE
    places = jnp.where(alive, rank, LIVE)
    return table.astype(jnp.int32), slots.astype(jnp.int32), places.astype(jnp.int32)


def body(features, cotangent, weight, occupancy, neighbours, first_moment, second_moment):
    channels = features.shape[3]
    capacity = features.shape[1]
    spatial = lax.axis_size("space")
    position = lax.axis_index("space")
    width = channels // spatial
    pad = ((0, 0), (0, 0), (0, LANES - width))
    table, slots, places = live_tables(neighbours[0])
    own = lax.dynamic_slice_in_dim(occupancy[0], position * capacity, capacity, 0)
    mask = own.astype(jnp.bfloat16)[:, :, None]

    narrow = lax.dynamic_slice_in_dim(weight, position * width, width, 1)
    narrow = jnp.pad(narrow, ((0, CHUNK - narrow.shape[0]), (0, LANES - width)))
    cot = (cotangent[0] * mask).reshape(capacity, 512, spatial, width)
    cot = jnp.pad(cot.transpose(2, 0, 1, 3), ((0, 0),) + pad)
    summed, back = step_call(table, slots, places, narrow, features[0] * mask, cot)
    summed = summed[: weight.shape[0], :width]
    back = back * own.astype(jnp.float32)[:, :, None]
    input_grad = (cotangent[0].astype(jnp.float32) + back).astype(jnp.bfloat16)[None]

    scaled = summed / 64.0
    new_first = 0.9 * first_moment + 0.1 * scaled
    new_second = 0.999 * second_moment + 0.001 * scaled * scaled
    return input_grad, new_first, new_second


def solution(mesh):
    return jax.shard_map(
        body,
        mesh=mesh,
        in_specs=(
            P("dp", "space", None, None),
            P("dp", "space", None, None),
            P("dp", None),
            P("dp", None, None),
            P("dp", None, None),
            P("dp", "space"),
            P("dp", "space"),
        ),
        out_specs=(P("dp", "space", None, None), P("dp", "space"), P("dp", "space")),
        check_vma=False,
    )
```

time: 131 us -> 114 us (0.87); the launches traced: 129 us -> 114 us
  Pallas kernels: 115 us -> 98.3 us
  other arithmetic: 7.31 us -> 9.21 us
    pallas_call x4 -> x1, Pallas kernels: 115 us -> 98.3 us  [step_call(): pl.pallas_call(step_kernel, out_shape=(jax.ShapeDtypeStruct((CHUNK, LANES...]
    unnamed x17 -> x15, local copies, waits for them, and re-layouts: 3.22 us -> 3.22 us
where the time goes in v2:
time: 114 us
  Pallas kernels  98.3 us (86%)
  other arithmetic  9.21 us (8%)
  local copies, waits for them, and re-layouts  5.8 us (5%)
    pallas_call x1, Pallas kernels, step_call(): pl.pallas_call(step_kernel, out_shape=(jax.ShapeDtypeStruct((CHUNK, LANES...  98.3 us
    unnamed x15, local copies, waits for them, and re-layouts  3.22 us
    broadcast_in_dim x1, other arithmetic, body(): (cotangent[0].astype(jnp.float32) + back).astype(jnp.bfloat16)[None]  2.55 us

profile of v2, /device:TPU:1, one launch (start us, length us, event | category | flops | bytes accessed | tf_op | source)
XLA Modules:
  0.0 114.0 jit_solution(969733825974587697)
XLA Ops:
  0.6 0.0 copy-start
  0.6 0.9 fusion.3
  1.6 0.1 convert_reduce_fusion
  1.7 0.8 multiply_reduce_fusion
  2.5 0.5 broadcast_select_fusion
  3.0 0.1 select_reduce_fusion
  3.1 0.6 broadcast_add_fusion.table
  3.7 0.7 convert_bitcast_fusion
  4.4 1.4 %copy.20 = bf16[1,2,512,384]{2,3,1,0:T(8,128)(2,1)S(1)} copy(bf16[1,2,512,384]{3,2,1,0:T(8,128)(2,1)} %param.8) | data formatting | bytes 1572864 | tf_op args[1]
  5.8 0.7 copy.21
  6.5 0.2 multiply_bitcast_fusion
  6.7 0.0 copy-start.2
  6.7 1.2 %pad.9.cot_own = bf16[4,2,512,128]{3,2,1,0:T(8,128)(2,1)} pad(bf16[4,2,512,96]{3,2,1,0:T(8,128)(2,1)S(1)} %multiply_bitcast_fusion, bf16[]{:T(256)} %constant.13.clone.1), padding=0_0x0_0x0_0x0_32 | pad | bytes 1835010 | tf_op jit(solution)/shard_map/jit(_pad)/pad | solution.py:439
  7.8 0.0 copy-done.2
  7.8 1.1 bitcast_multiply_fusion.feat_own
  8.9 0.7 select_reduce_fusion.1.slots
  9.6 0.0 copy-done
  9.6 0.1 constant_dynamic-slice_fusion
  9.7 0.7 pad.8.rows
  10.4 0.0 copy-start.3
  10.4 0.0 copy-start.4
  10.4 98.3 %shard_map.94 = (f32[336,128]{1,0:T(8,128)}, f32[2,512,384]{2,1,0:T(8,128)}) custom-call(s32[4,27]{1,0:T(4,128)} %broadcast_add_fusion.table, s32[4]{0:T(128)} %select_reduce_fusion.1.slots, s32[8]{0:T(128)} %get-tuple-element.20.places, bf16[336,128]{1,0:T(8,128)(2,1)} %pad.8.rows, bf16[2,512,384]{2,1,0:T(8,128)(2,1)} %bitcast_multiply_fusion.feat_own, ...), custom_call_target="tpu_custom_call" | custom-call | flops 16307453952 | bytes 10000000 | tf_op jit(solution)/shard_map/pallas_call | solution.py:365
  108.6 0.0 copy-start.1
  108.7 0.0 copy-done.3
  108.7 0.1 copy.22
  108.8 0.0 copy-done.4
  108.8 0.1 copy.23
  108.9 1.0 multiply_add_fusion
  109.9 0.8 copy.24
  110.7 0.8 copy.25
  111.5 0.0 copy-done.1
  111.5 2.5 %fusion.1 = bf16[1,2,512,384]{3,2,1,0:T(8,128)(2,1)} fusion(f32[2,512,384]{2,1,0:T(8,128)} %get-tuple-element.5, bf16[1,2,512,384]{3,2,1,0:T(8,128)(2,1)S(1)} %copy-done.1, f32[2,512]{1,0:T(2,128)S(1)} %get-tuple-element.18), kind=kLoop, calls=%fused_computation.3 | loop fusion | flops 1572864 | bytes 3149824 | tf_op jit(solution)/shard_map/broadcast_in_dim | solution.py:443
  (1 shorter events, 0.0 us)
Async XLA Ops:
  0.6 9.0 %copy-start = (bf16[324,384]{1,0:T(8,128)(2,1)S(1)}, bf16[324,384]{1,0:T(8,128)(2,1)}, u32[]{:S(2)}) copy-start(bf16[324,384]{1,0:T(8,128)(2,1)} %param.9) | copy-start | bytes 746500
  6.7 1.2 %copy-start.2 = (bf16[1,2,512,384]{3,2,1,0:T(8,128)(2,1)S(1)}, bf16[1,2,512,384]{3,2,1,0:T(8,128)(2,1)}, u32[]{:S(2)}) copy-start(bf16[1,2,512,384]{3,2,1,0:T(8,128)(2,1)} %param.7) | copy-start | bytes 2359300
  10.4 98.3 %copy-start.3 = (f32[324,96]{0,1:T(8,128)S(1)}, f32[324,96]{0,1:T(8,128)}, u32[]{:S(2)}) copy-start(f32[324,96]{0,1:T(8,128)} %param.12) | copy-start | bytes 373252
  10.4 98.4 %copy-start.4 = (f32[324,96]{0,1:T(8,128)S(1)}, f32[324,96]{0,1:T(8,128)}, u32[]{:S(2)}) copy-start(f32[324,96]{0,1:T(8,128)} %param.13) | copy-start | bytes 373252
  108.6 2.8 %copy-start.1 = (bf16[1,2,512,384]{3,2,1,0:T(8,128)(2,1)S(1)}, bf16[1,2,512,384]{3,2,1,0:T(8,128)(2,1)}, u32[]{:S(2)}) copy-start(bf16[1,2,512,384]{3,2,1,0:T(8,128)(2,1)} %param.8) | copy-start | bytes 2359300

commit v3 on v2

--- a/solution.py
+++ b/solution.py
@@ -69,11 +69,13 @@
     def step(self, axis, by):
         return self.at(**{axis: (getattr(self, axis) + by) % 4})
 
-    def meet(self, others):
+    def greet(self, others):
         barrier = pltpu.get_barrier_semaphore()
         for other in others:
             pl.semaphore_signal(barrier, inc=1, device_id=other, device_id_type=MESH)
-        pl.semaphore_wait(barrier, len(others))
+
+    def met(self, others):
+        pl.semaphore_wait(pltpu.get_barrier_semaphore(), len(others))
 
     def everyone(self):
         return (
@@ -183,16 +185,57 @@
             out[half] = total.astype(out.dtype)
 
 
+def read_links(links, chip, table, slots, place, order, inward, onward):
+    group = links.shape[1]
+    alive = [(links[0, s, 13] >= 0).astype(jnp.int32) for s in range(group)]
+    near = [(chip == s // (group // 2)).astype(jnp.int32) for s in range(group)]
+    others = sum(a * (1 - n) for a, n in zip(alive, near))
+    rank, counts, position = [], [0, 0], []
+    total = 0
+    for s in range(group):
+        side = s // (group // 2)
+        rank.append(total)
+        position.append(counts[side] + near[s] * others)
+        place[s + 1] = jnp.where(alive[s] > 0, jnp.minimum(total, LIVE), LIVE)
+        inward[s] = jnp.where(alive[s] > 0, jnp.minimum(counts[side], LIVE), LIVE)
+        onward[s] = jnp.where(alive[s] > 0, jnp.minimum(position[s], LIVE), LIVE)
+        total = total + alive[s]
+        counts[side] = counts[side] + alive[s]
+    place[0] = LIVE
+    for r in range(LIVE):
+        slots[r] = sum(jnp.where(rank[s] == r, alive[s] * s, 0) for s in range(group))
+        turn = sum(jnp.where(position[s] == r, alive[s] * rank[s], 0) for s in range(group))
+        order[r] = jnp.minimum(turn, LIVE - 1)
+
+    def code_of(code, carry):
+        for r in range(LIVE):
+            table[r, code] = place[links[0, slots[r], code] + 1]
+        return carry
+
+    lax.fori_loop(0, 27, code_of, 0)
+
+
+def lanes_from(values, start, width):
+    turned = pltpu.roll(values, (values.shape[1] - start) % values.shape[1], 1)[:, :LANES]
+    lane = lax.broadcasted_iota(jnp.int32, turned.shape, 1)
+    return jnp.where(lane < width, turned, 0.0).astype(jnp.bfloat16)
+
+
 def step_kernel(
-    table, slots, places, rows, feat_own, cot_own, grad, total,
-    parts, feat, cot, blocks, regions, delta, delta_t, stage, weight, thin, back_live, back,
+    links, occupancy, features, cotangent, shard, input_grad, grad,
+    rows, cot_own, mask, table, slots, place, order, inward, onward,
+    parts, feat, cot, blocks, regions, delta, delta_t, stage, weight, thin,
     a_near, a_left, a_right, b_near, b_left, b_right, a_mid, b_mid,
-    c_near, c_left, c_right, d_near, d_left, d_right, last, from_z, from_core, to_chip, from_chip,
+    c_near, c_left, c_right, d_near, d_left, d_right, last, from_z,
+    halves, inbox, chip_sum, z_out, z_in, fin_out, fin_in,
     local_sem, send_sem, recv_sem,
 ):
-    live, group = slots.shape[0], places.shape[0]
-    capacity, channels = feat_own.shape[0], feat_own.shape[2]
-    rows_of = 27 * channels // 32
+    live, group = LIVE, links.shape[1]
+    capacity, voxels, channels = features.shape[1:]
+    spatial = group // capacity
+    width = channels // spatial
+    rows_of = shard.shape[0]
+    half = voxels // 2
     w = Wires(send_sem, recv_sem)
     x, y, z, chip, core = w.x, w.y, w.z, w.chip, w.core
     me, over, beside = chip * 2 + core, (1 - chip) * 2 + core, chip * 2 + 1 - core
@@ -209,24 +252,40 @@
     sum_b = RingReduce(w, "x", lambda q, h: parts.at[h, q, :, CUT:], b_near, b_left, b_right)
     end_a = RingReduce(w, "x", lambda q, h: a_mid.at[h, q], c_near, c_left, c_right)
     end_b = RingReduce(w, "y", lambda q, h: b_mid.at[h, q], d_near, d_left, d_right)
-    t_out, t_far, t_own, t_chip = (w.ticket() for _ in range(4))
-
-    w.meet(w.everyone())
+    t_out, t_fin = w.ticket(), w.ticket()
+    t_core = [w.ticket() for _ in range(live)]
+    t_chip = [w.ticket() for _ in range(live)]
+
+    w.greet(w.everyone())
+    rows[CHUNK - 16 :] = jnp.zeros((16, LANES), jnp.bfloat16)
+    start = (spatial - me) % spatial * width
+    turned = pltpu.roll(shard[...].astype(jnp.float32), start, 1)[:, :LANES]
+    lane = lax.broadcasted_iota(jnp.int32, turned.shape, 1)
+    rows[:rows_of] = jnp.where(lane < width, turned, 0.0).astype(jnp.bfloat16)
+    w.met(w.everyone())
     w.send(t_z, rows, parts.at[z, x, y], w.at(z=1 - z))
-    w.send(t_over, feat_own, feat.at[me], to_over)
-    w.send(t_beside, feat_own, feat.at[me], to_beside)
-    w.send(c_beside, cot_own.at[beside], cot.at[me], to_beside)
+    w.send(t_over, features.at[0], feat.at[me], to_over)
+    w.send(t_beside, features.at[0], feat.at[me], to_beside)
     keep = [
         pltpu.make_async_copy(rows, parts.at[z, x, y], local_sem.at[0]),
-        pltpu.make_async_copy(feat_own, feat.at[me], local_sem.at[1]),
-        pltpu.make_async_copy(cot_own.at[me], cot.at[me], local_sem.at[2]),
+        pltpu.make_async_copy(features.at[0], feat.at[me], local_sem.at[1]),
     ]
     for copy in keep:
         copy.start()
+    read_links(links, chip, table, slots, place, order, inward, onward)
     keep[0].wait()
     w.arrived(t_z, parts.at[1 - z, x, y])
     first_a.start()
     first_b.start()
+    for s in range(spatial):
+        for n in range(capacity):
+            cot_own[s, n] = lanes_from(cotangent[0, n].astype(jnp.float32), s * width, width)
+    cot[me] = cot_own[me]
+    w.send(c_beside, cot_own.at[beside], cot.at[me], to_beside)
+    held = occupancy[0].astype(jnp.float32)
+    held = jnp.concatenate([held] * (LANES // group), axis=0).T
+    for s in range(group):
+        mask[s] = jnp.broadcast_to(held[:, s : s + 1], (voxels, LANES))
     first_a.forward()
     first_b.forward()
     first_a.end()
@@ -240,14 +299,13 @@
     last_a.forward()
     last_b.forward()
     keep[1].wait()
-    keep[2].wait()
     w.arrived(t_beside, feat.at[beside])
     w.arrived(t_across, feat.at[across])
 
     for r in range(live):
-        blocks[r] = feat[slots[r] // capacity, slots[r] % capacity].astype(jnp.float32).reshape(
-            64, 8, channels
-        )
+        full = jnp.concatenate([mask[slots[r]]] * (channels // LANES), axis=1)
+        field = feat[slots[r] // capacity, slots[r] % capacity].astype(jnp.float32)
+        blocks[r] = (field * full).reshape(64, 8, channels)
     blocks[live] = jnp.zeros((64, 8, channels), jnp.float32)
     fill_regions(table, blocks, regions, live)
     last_a.end()
@@ -272,7 +330,7 @@
             pre = pre + jnp.dot(lhs, rhs, preferred_element_type=jnp.float32)
         gate = jax.nn.sigmoid(pre)
         value = cot[slots[r] // capacity, slots[r] % capacity].astype(jnp.float32)
-        delta[r] = (value * gate * (1.0 + pre * (1.0 - gate))).astype(jnp.bfloat16)
+        delta[r] = (value * mask[slots[r]] * gate * (1.0 + pre * (1.0 - gate))).astype(jnp.bfloat16)
         return carry
 
     lax.fori_loop(0, live, forward_block, 0)
@@ -299,10 +357,13 @@
     thin[live] = jnp.zeros((64, 8, LANES), jnp.float32)
     narrow = regions.at[:, :, :, :, :LANES]
     fill_regions(table, thin, narrow, live)
-    back_live[live] = jnp.zeros((512, channels), jnp.bfloat16)
-
-    def back_block(r, carry):
-        out = jnp.zeros((512, channels), jnp.float32)
+
+    chip_sum[live] = jnp.zeros((half, channels), jnp.float32)
+    z_in[live] = jnp.zeros((half, channels), jnp.bfloat16)
+
+    def back_block(j):
+        r = order[j]
+        out = jnp.zeros((voxels, channels), jnp.float32)
         for ks in (range(g, min(g + 4, 27)) for g in range(0, 27, 4)):
             lhs = jnp.concatenate([shifted_rows(narrow, r, 26 - k, LANES) for k in ks], axis=1)
             rhs = jnp.concatenate(
@@ -311,45 +372,69 @@
             out = out + lax.dot_general(
                 lhs, rhs, (((1,), (1,)), ((), ())), preferred_element_type=jnp.float32
             )
-        back_live[r] = out.astype(jnp.bfloat16)
-        return carry
-
-    lax.fori_loop(0, live // 2, back_block, 0)
+        halves[j] = out.astype(jnp.bfloat16).reshape(2, half, channels)
+        w.send(t_core[j], halves.at[j, 1 - core], inbox.at[j], to_beside)
+
+    def join(j):
+        w.arrived(t_core[j], inbox.at[j])
+        value = halves[j, core].astype(jnp.float32) + inbox[j].astype(jnp.float32)
+        chip_sum[j] = value
+        z_out[j] = value.astype(jnp.bfloat16)
+        w.send(t_chip[j], z_out.at[j], z_in.at[j], to_over)
+
+    back_block(0)
+    back_block(1)
+    join(0)
     sum_a.forward()
     sum_b.forward()
-    lax.fori_loop(live // 2, live, back_block, 0)
-    for slot in range(group):
-        back[slot // capacity, slot % capacity] = back_live[places[slot]]
-    w.send(t_far, back.at[across], from_core.at[1 - chip], to_beside)
-    w.send(t_own, back.at[beside], from_core.at[chip], to_beside)
+    back_block(2)
+    join(1)
+    back_block(3)
+    join(2)
     sum_a.end(a_mid)
     sum_b.end(b_mid)
     end_a.start()
     end_b.start()
-    w.arrived(t_far, from_core.at[1 - chip])
-    to_chip[...] = (
-        back[over].astype(jnp.float32) + from_core[1 - chip].astype(jnp.float32)
-    ).astype(jnp.bfloat16)
-    w.send(t_chip, to_chip, from_chip, to_over)
+    join(3)
     end_a.forward()
     end_b.forward()
-    w.arrived(t_own, from_core.at[chip])
-    total[...] = back[me].astype(jnp.float32) + from_core[chip].astype(jnp.float32)
     end_a.end(last.at[:, :CUT])
     end_b.end(last.at[:, CUT:])
     w.send(t_out, last.at[1 - z], from_z, w.at(z=1 - z))
+    for j in range(live):
+        w.arrived(t_chip[j], z_in.at[j])
+
+    def whole(owner, n):
+        s = owner * capacity + n
+        return z_in[inward[s]].astype(jnp.float32) + chip_sum[onward[s]]
+
+    def finish(n, part, value):
+        span = pl.ds(pl.multiple_of(part * half, half), half)
+        full = jnp.concatenate([mask[me * capacity + n, span]] * (channels // LANES), axis=1)
+        value = cotangent[0, n, span].astype(jnp.float32) + full * value
+        input_grad[0, n, span] = value.astype(jnp.bfloat16)
+
+    for n in range(capacity):
+        fin_out[n] = whole(beside, n).astype(jnp.bfloat16)
+    w.send(t_fin, fin_out, fin_in, to_beside)
+    for n in range(capacity):
+        finish(n, core, whole(me, n))
     w.arrived(t_out, from_z)
-    grad[...] = last[z].astype(jnp.float32) + from_z[...].astype(jnp.float32)
-    w.arrived(t_chip, from_chip)
-    total[...] = total[...] + from_chip[...].astype(jnp.float32)
+    done = last[z].astype(jnp.float32) + from_z[...].astype(jnp.float32)
+    fill = jnp.zeros((grad.shape[1] - CHUNK, LANES), jnp.float32)
+    grad[...] = jnp.concatenate([done, fill], axis=0).T
+    w.arrived(t_fin, fin_in)
+    for n in range(capacity):
+        finish(n, 1 - core, fin_in[n].astype(jnp.float32))
     w.finish()
 
 
-def step_call(table, slots, places, rows, feat_own, cot_own):
-    live, spatial = slots.shape[0], cot_own.shape[0]
-    channels = feat_own.shape[2]
+def step_call(links, occupancy, features, cotangent, shard):
+    live, group = LIVE, links.shape[1]
+    capacity, voxels, channels = features.shape[1:]
+    spatial, half = group // capacity, voxels // 2
     rest = CHUNK - CUT
-    copies = 8 * 6 + 11
+    copies = 8 * 6 + 9 + 2 * live
 
     def buffer(*shape):
         return pltpu.VMEM(shape, jnp.bfloat16)
@@ -360,29 +445,39 @@
     def ring(*shape):
         return [buffer(2, *shape, LANES)] * 3
 
-    block = feat_own.shape
-    flops = 3 * 2 * live * 512 * 27 * channels * LANES
+    def scalars(*shape):
+        return pltpu.SMEM(shape, jnp.int32)
+
+    block = (capacity, voxels, channels)
+    flops = 3 * 2 * live * voxels * 27 * channels * LANES
     return pl.pallas_call(
         step_kernel,
         out_shape=(
-            jax.ShapeDtypeStruct((CHUNK, LANES), jnp.float32),
-            jax.ShapeDtypeStruct(block, jnp.float32),
+            jax.ShapeDtypeStruct(features.shape, jnp.bfloat16),
+            jax.ShapeDtypeStruct((LANES, 3 * LANES), jnp.float32),
         ),
-        in_specs=[SMEM_SPEC] * 3 + [VMEM_SPEC] * 3,
+        in_specs=[SMEM_SPEC] + [VMEM_SPEC] * 4,
         out_specs=(VMEM_SPEC,) * 2,
         scratch_shapes=[
+            buffer(CHUNK, LANES),
+            buffer(spatial, capacity, voxels, LANES),
+            wide(group, voxels, LANES),
+            scalars(live, 27),
+            scalars(live),
+            scalars(group + 1),
+            scalars(live),
+            scalars(group),
+            scalars(group),
             buffer(2, 4, 4, CHUNK, LANES),
             buffer(spatial, *block),
-            buffer(*cot_own.shape),
+            buffer(spatial, capacity, voxels, LANES),
             wide(live + 1, 64, 8, channels),
             buffer(9, live, 10, 64, channels),
-            buffer(live, 512, LANES),
-            buffer(LANES, live * 512),
+            buffer(live, voxels, LANES),
+            buffer(LANES, live * voxels),
             wide(27 * channels + 16, LANES),
             buffer(27 * channels, LANES),
             wide(live + 1, 64, 8, LANES),
-            buffer(live + 1, 512, channels),
-            buffer(spatial, *block),
         ]
         + ring(4, CUT)
         + ring(4, rest)
@@ -392,10 +487,14 @@
         + [
             buffer(2, CHUNK, LANES),
             buffer(CHUNK, LANES),
-            buffer(2, *block),
-            buffer(*block),
-            buffer(*block),
-            pltpu.SemaphoreType.DMA((3,)),
+            buffer(live, 2, half, channels),
+            buffer(live, half, channels),
+            wide(live + 1, half, channels),
+            buffer(live, half, channels),
+            buffer(live + 1, half, channels),
+            buffer(capacity, half, channels),
+            buffer(capacity, half, channels),
+            pltpu.SemaphoreType.DMA((2,)),
             pltpu.SemaphoreType.DMA((copies,)),
             pltpu.SemaphoreType.DMA((copies,)),
         ],
@@ -403,49 +502,15 @@
             collective_id=0, has_side_effects=True, vmem_limit_bytes=VMEM_BYTES
         ),
         cost_estimate=pl.CostEstimate(flops=flops, bytes_accessed=10**7, transcendentals=10**6),
-    )(table, slots, places, rows, feat_own, cot_own)
-
-
-def live_tables(links):
-    group = links.shape[0]
-    alive = links[:, 13] >= 0
-    order = jnp.arange(group, dtype=jnp.int32)
-    before = (order[None, :] < order[:, None]) & alive[None, :]
-    rank = jnp.sum(before.astype(jnp.int32), axis=1)
-    places = jnp.arange(LIVE, dtype=jnp.int32)
-    chosen = ((rank[None, :] == places[:, None]) & alive[None, :]).astype(jnp.int32)
-    slots = jnp.sum(chosen * jnp.arange(group, dtype=jnp.int32)[None, :], axis=1)
-    rows = jnp.sum(chosen[:, :, None] * links[None, :, :], axis=1)
-    named = (rows[:, :, None] == jnp.arange(group, dtype=jnp.int32)).astype(jnp.int32)
-    table = jnp.sum(named * (rank - LIVE)[None, None, :], axis=2) + LIVE
-    places = jnp.where(alive, rank, LIVE)
-    return table.astype(jnp.int32), slots.astype(jnp.int32), places.astype(jnp.int32)
+    )(links, occupancy, features, cotangent, shard)
 
 
 def body(features, cotangent, weight, occupancy, neighbours, first_moment, second_moment):
-    channels = features.shape[3]
-    capacity = features.shape[1]
-    spatial = lax.axis_size("space")
-    position = lax.axis_index("space")
-    width = channels // spatial
-    pad = ((0, 0), (0, 0), (0, LANES - width))
-    table, slots, places = live_tables(neighbours[0])
-    own = lax.dynamic_slice_in_dim(occupancy[0], position * capacity, capacity, 0)
-    mask = own.astype(jnp.bfloat16)[:, :, None]
-
-    narrow = lax.dynamic_slice_in_dim(weight, position * width, width, 1)
-    narrow = jnp.pad(narrow, ((0, CHUNK - narrow.shape[0]), (0, LANES - width)))
-    cot = (cotangent[0] * mask).reshape(capacity, 512, spatial, width)
-    cot = jnp.pad(cot.transpose(2, 0, 1, 3), ((0, 0),) + pad)
-    summed, back = step_call(table, slots, places, narrow, features[0] * mask, cot)
-    summed = summed[: weight.shape[0], :width]
-    back = back * own.astype(jnp.float32)[:, :, None]
-    input_grad = (cotangent[0].astype(jnp.float32) + back).astype(jnp.bfloat16)[None]
-
-    scaled = summed / 64.0
-    new_first = 0.9 * first_moment + 0.1 * scaled
-    new_second = 0.999 * second_moment + 0.001 * scaled * scaled
-    return input_grad, new_first, new_second
+    input_grad, summed = step_call(neighbours, occupancy, features, cotangent, weight)
+    scaled = summed[: first_moment.shape[1], : first_moment.shape[0]] / 64.0
+    new_first = 0.9 * first_moment.T + 0.1 * scaled
+    new_second = 0.999 * second_moment.T + 0.001 * scaled * scaled
+    return input_grad, new_first.T, new_second.T
 
 
 def solution(mesh):

time: 114 us -> 94.3 us (0.83)
  Pallas kernels: 98.3 us -> 89.6 us
  other arithmetic: 9.21 us -> 1.67 us
  local copies, waits for them, and re-layouts: 5.8 us -> 2.1 us
    pallas_call x1, Pallas kernels: 98.3 us -> 89.6 us  [step_call(): pl.pallas_call(step_kernel, out_shape=(jax.ShapeDtypeStruct(features.shap...]
    broadcast_in_dim x1 -> x0, other arithmetic: 2.55 us -> none  [body(): (cotangent[0].astype(jnp.float32) + back).astype(jnp.bfloat16)[None]]
    pad x2 -> x0, local copies, waits for them, and re-layouts: 1.83 us -> none  [the longest x1 1.17 us: body(): cot = jnp.pad(cot.transpose(2, 0, 1, 3), ((0, 0),) + pad)]
    reduce_sum x4 -> x0, other arithmetic: 1.64 us -> none  [the longest x1 0.78 us: live_tables(): rows = jnp.sum(chosen[:, :, None] * links[None, :, :], axis=1)]
    add x2 -> x0, other arithmetic: 1.57 us -> none  [the longest x1 0.98 us: body(): new_second = 0.999 * second_moment + 0.001 * scaled * scaled]
    transpose x1, other arithmetic: 0.2 us -> 1.67 us  [body(): return (input_grad, new_first.T, new_second.T)]
    unnamed x15 -> x5, local copies, waits for them, and re-layouts: 3.22 us -> 2.1 us
where the time goes in v3:
time: 94.3 us; the launch traced here: 94 us
  Pallas kernels  89.6 us (95%)
  local copies, waits for them, and re-layouts  2.1 us (2%)
  other arithmetic  1.67 us (2%)
    pallas_call x1, Pallas kernels, step_call(): pl.pallas_call(step_kernel, out_shape=(jax.ShapeDtypeStruct(features.shap...  89.6 us
    unnamed x5, local copies, waits for them, and re-layouts  2.1 us

profile of v3, /device:TPU:1, one launch (start us, length us, event | category | flops | bytes accessed | tf_op | source)
XLA Modules:
  0.0 94.0 jit_solution(15783439338791028354)
XLA Ops:
  0.6 0.0 copy-start
  0.6 0.0 copy-start.1
  0.7 89.6 %shard_map.94 = (bf16[1,2,512,384]{3,2,1,0:T(8,128)(2,1)}, f32[128,384]{1,0:T(8,128)}) custom-call(s32[1,8,27]{2,1,0:T(8,128)} %links.1, s32[1,8,512]{2,1,0:T(8,128)} %occupancy.1, bf16[1,2,512,384]{3,2,1,0:T(8,128)(2,1)} %features.1, bf16[1,2,512,384]{3,2,1,0:T(8,128)(2,1)} %cotangent.1, bf16[324,384]{1,0:T(8,128)(2,1)} %shard.1), custom_call_target="tpu_custom_call" | custom-call | flops 16307453952 | bytes 10000000 | tf_op jit(solution)/shard_map/pallas_call | solution.py:453
  90.3 0.0 copy-done
  90.3 0.0 copy-done.1
  90.3 1.7 %fusion = (f32[324,96]{0,1:T(8,128)}, f32[324,96]{0,1:T(8,128)}) fusion(f32[324,96]{0,1:T(8,128)S(1)} %copy-done, f32[128,384]{1,0:T(8,128)} %get-tuple-element.6, f32[324,96]{0,1:T(8,128)S(1)} %copy-done.1), kind=kLoop, calls=%fused_computation.1 | loop fusion | flops 248832 | bytes 622080 | tf_op jit(solution)/shard_map/transpose | solution.py:513
  91.9 2.1 %copy.11 = bf16[1,2,512,384]{3,2,1,0:T(8,128)(2,1)} copy(bf16[1,2,512,384]{3,2,1,0:T(8,128)(2,1)} %get-tuple-element.12) | data formatting | bytes 1572864
Async XLA Ops:
  0.6 89.6 %copy-start = (f32[324,96]{0,1:T(8,128)S(1)}, f32[324,96]{0,1:T(8,128)}, u32[]{:S(2)}) copy-start(f32[324,96]{0,1:T(8,128)} %param.13) | copy-start | bytes 373252
  0.6 89.6 %copy-start.1 = (f32[324,96]{0,1:T(8,128)S(1)}, f32[324,96]{0,1:T(8,128)}, u32[]{:S(2)}) copy-start(f32[324,96]{0,1:T(8,128)} %param.12) | copy-start | bytes 373252

commit v4 on v3

--- a/solution.py
+++ b/solution.py
@@ -215,16 +215,14 @@
     lax.fori_loop(0, 27, code_of, 0)
 
 
-def lanes_from(values, start, width):
-    turned = pltpu.roll(values, (values.shape[1] - start) % values.shape[1], 1)[:, :LANES]
-    lane = lax.broadcasted_iota(jnp.int32, turned.shape, 1)
-    return jnp.where(lane < width, turned, 0.0).astype(jnp.bfloat16)
+def lanes_from(values, start):
+    return pltpu.roll(values, (values.shape[1] - start) % values.shape[1], 1)[:, :LANES]
 
 
 def step_kernel(
     links, occupancy, features, cotangent, shard, input_grad, grad,
     rows, cot_own, mask, table, slots, place, order, inward, onward,
-    parts, feat, cot, blocks, regions, delta, delta_t, stage, weight, thin,
+    parts, feat, cot, blocks, regions, delta_t, stage, weight, weight_t, thin,
     a_near, a_left, a_right, b_near, b_left, b_right, a_mid, b_mid,
     c_near, c_left, c_right, d_near, d_left, d_right, last, from_z,
     halves, inbox, chip_sum, z_out, z_in, fin_out, fin_in,
@@ -279,7 +277,8 @@
     first_b.start()
     for s in range(spatial):
         for n in range(capacity):
-            cot_own[s, n] = lanes_from(cotangent[0, n].astype(jnp.float32), s * width, width)
+            some = lanes_from(cotangent[0, n].astype(jnp.float32), s * width)
+            cot_own[s, n] = some.T[:width].astype(jnp.bfloat16)
     cot[me] = cot_own[me]
     w.send(c_beside, cot_own.at[beside], cot.at[me], to_beside)
     held = occupancy[0].astype(jnp.float32)
@@ -315,34 +314,41 @@
             jnp.float32
         )
     for k in range(27):
-        weight[k * channels : (k + 1) * channels] = stage[
-            pl.ds(k, channels, stride=27), :
-        ].astype(jnp.bfloat16)
+        some = stage[pl.ds(k, channels, stride=27), :]
+        weight[k * channels : (k + 1) * channels] = some.astype(jnp.bfloat16)
+        weight_t[:, k * channels : (k + 1) * channels] = some.T[:width].astype(jnp.bfloat16)
     w.arrived(c_over, cot.at[over])
     w.arrived(c_beside, cot.at[beside])
     w.arrived(c_across, cot.at[across])
 
-    def forward_block(r, carry):
-        pre = jnp.zeros((512, LANES), jnp.float32)
+    def forward_block(r):
+        pre = jnp.zeros((width, voxels), jnp.float32)
         for ks in (range(g, min(g + 2, 27)) for g in range(0, 27, 2)):
-            lhs = jnp.concatenate([shifted_rows(regions, r, k, channels) for k in ks], axis=1)
-            rhs = weight[ks[0] * channels : (ks[-1] + 1) * channels]
-            pre = pre + jnp.dot(lhs, rhs, preferred_element_type=jnp.float32)
+            field = jnp.concatenate([shifted_rows(regions, r, k, channels) for k in ks], axis=1)
+            lhs = weight_t[:, ks[0] * channels : (ks[-1] + 1) * channels]
+            pre = pre + lax.dot_general(
+                lhs, field, (((1,), (1,)), ((), ())), preferred_element_type=jnp.float32
+            )
         gate = jax.nn.sigmoid(pre)
         value = cot[slots[r] // capacity, slots[r] % capacity].astype(jnp.float32)
-        delta[r] = (value * mask[slots[r]] * gate * (1.0 + pre * (1.0 - gate))).astype(jnp.bfloat16)
-        return carry
-
-    lax.fori_loop(0, live, forward_block, 0)
+        value = value * occupancy[0, pl.ds(slots[r], 1)].astype(jnp.float32)
+        value = (value * gate * (1.0 + pre * (1.0 - gate))).astype(jnp.bfloat16)
+        delta_t[:, r * voxels : (r + 1) * voxels] = value
+        value = jnp.concatenate(
+            [value.astype(jnp.float32), jnp.zeros((LANES - width, voxels), jnp.float32)], axis=0
+        )
+        thin[r] = value.T.reshape(64, 8, LANES)
+
     for r in range(live):
-        delta_t[:, r * 512 : (r + 1) * 512] = (
-            delta[r].astype(jnp.float32).T.astype(jnp.bfloat16)
-        )
+        forward_block(r)
     for k in range(27):
         field = jnp.concatenate(
             [shifted_rows(regions, r, k, channels) for r in range(live)], axis=0
         )
         part = jnp.dot(delta_t[...], field, preferred_element_type=jnp.float32)
+        part = jnp.concatenate(
+            [part, jnp.zeros((LANES - width, channels), jnp.float32)], axis=0
+        )
         stage[pl.ds(k, channels, stride=27), :] = part.T
     w.finish()
     for d in range(32):
@@ -352,8 +358,6 @@
     sum_a.start()
     sum_b.start()
 
-    for r in range(live):
-        thin[r] = delta[r].astype(jnp.float32).reshape(64, 8, LANES)
     thin[live] = jnp.zeros((64, 8, LANES), jnp.float32)
     narrow = regions.at[:, :, :, :, :LANES]
     fill_regions(table, thin, narrow, live)
@@ -460,7 +464,7 @@
         out_specs=(VMEM_SPEC,) * 2,
         scratch_shapes=[
             buffer(CHUNK, LANES),
-            buffer(spatial, capacity, voxels, LANES),
+            buffer(spatial, capacity, channels // spatial, voxels),
             wide(group, voxels, LANES),
             scalars(live, 27),
             scalars(live),
@@ -470,13 +474,13 @@
             scalars(group),
             buffer(2, 4, 4, CHUNK, LANES),
             buffer(spatial, *block),
-            buffer(spatial, capacity, voxels, LANES),
+            buffer(spatial, capacity, channels // spatial, voxels),
             wide(live + 1, 64, 8, channels),
             buffer(9, live, 10, 64, channels),
-            buffer(live, voxels, LANES),
-            buffer(LANES, live * voxels),
+            buffer(channels // spatial, live * voxels),
             wide(27 * channels + 16, LANES),
             buffer(27 * channels, LANES),
+            buffer(channels // spatial, 27 * channels),
             wide(live + 1, 64, 8, LANES),
         ]
         + ring(4, CUT)

time: 94.3 us -> 91.7 us (0.972)
  Pallas kernels: 89.6 us -> 87.1 us
    pallas_call x1, Pallas kernels: 89.6 us -> 87.1 us  [step_call(): pl.pallas_call(step_kernel, out_shape=(jax.ShapeDtypeStruct(features.shap...]
where the time goes in v4:
time: 91.7 us; the launch traced here: 91.5 us
  Pallas kernels  87.1 us (95%)
  local copies, waits for them, and re-layouts  2.1 us (2%)
  other arithmetic  1.67 us (2%)
    pallas_call x1, Pallas kernels, step_call(): pl.pallas_call(step_kernel, out_shape=(jax.ShapeDtypeStruct(features.shap...  87.1 us
    unnamed x5, local copies, waits for them, and re-layouts  2.1 us

profile of v4, /device:TPU:1, one launch (start us, length us, event | category | flops | bytes accessed | tf_op | source)
XLA Modules:
  0.0 91.5 jit_solution(13959969528973020956)
XLA Ops:
  0.6 0.0 copy-start
  0.6 0.0 copy-start.1
  0.7 87.1 %shard_map.94 = (bf16[1,2,512,384]{3,2,1,0:T(8,128)(2,1)}, f32[128,384]{1,0:T(8,128)}) custom-call(s32[1,8,27]{2,1,0:T(8,128)} %links.1, s32[1,8,512]{2,1,0:T(8,128)} %occupancy.1, bf16[1,2,512,384]{3,2,1,0:T(8,128)(2,1)} %features.1, bf16[1,2,512,384]{3,2,1,0:T(8,128)(2,1)} %cotangent.1, bf16[324,384]{1,0:T(8,128)(2,1)} %shard.1), custom_call_target="tpu_custom_call" | custom-call | flops 16307453952 | bytes 10000000 | tf_op jit(solution)/shard_map/pallas_call | solution.py:457
  87.7 0.0 copy-done
  87.7 0.0 copy-done.1
  87.8 1.7 %fusion = (f32[324,96]{0,1:T(8,128)}, f32[324,96]{0,1:T(8,128)}) fusion(f32[324,96]{0,1:T(8,128)S(1)} %copy-done, f32[128,384]{1,0:T(8,128)} %get-tuple-element.6, f32[324,96]{0,1:T(8,128)S(1)} %copy-done.1), kind=kLoop, calls=%fused_computation.1 | loop fusion | flops 248832 | bytes 622080 | tf_op jit(solution)/shard_map/transpose | solution.py:517
  89.4 2.1 %copy.11 = bf16[1,2,512,384]{3,2,1,0:T(8,128)(2,1)} copy(bf16[1,2,512,384]{3,2,1,0:T(8,128)(2,1)} %get-tuple-element.12) | data formatting | bytes 1572864
Async XLA Ops:
  0.6 87.1 %copy-start = (f32[324,96]{0,1:T(8,128)S(1)}, f32[324,96]{0,1:T(8,128)}, u32[]{:S(2)}) copy-start(f32[324,96]{0,1:T(8,128)} %param.13) | copy-start | bytes 373252
  0.6 87.1 %copy-start.1 = (f32[324,96]{0,1:T(8,128)S(1)}, f32[324,96]{0,1:T(8,128)}, u32[]{:S(2)}) copy-start(f32[324,96]{0,1:T(8,128)} %param.12) | copy-start | bytes 373252

commit v5 on v4

--- a/solution.py
+++ b/solution.py
@@ -120,69 +120,52 @@
     def __init__(self, wires, axis, block):
         self.wires, self.axis, self.block = wires, axis, block
         self.q = getattr(wires, axis)
-        self.tickets = [wires.ticket() for _ in range(6)]
-
-    def start(self):
-        t, q = self.tickets, self.q
-        right, left = self.wires.step(self.axis, 1), self.wires.step(self.axis, 3)
-        for ticket, half, other in ((t[0], 0, right), (t[1], 1, left), (t[2], 1, right), (t[3], 0, left)):
-            mine = self.block(q, half)
-            self.wires.send(ticket, mine, mine, other)
-
-    def forward(self):
-        t, q = self.tickets, self.q
-        right, left = self.wires.step(self.axis, 1), self.wires.step(self.axis, 3)
-        for ticket, into, half, source, other in (
-            (t[0], t[4], 0, (q + 3) % 4, right),
-            (t[1], t[5], 1, (q + 1) % 4, left),
-        ):
-            piece = self.block(source, half)
-            self.wires.arrived(ticket, piece)
-            self.wires.send(into, piece, piece, other)
-
-    def end(self):
-        t, q = self.tickets, self.q
-        self.wires.arrived(t[2], self.block((q + 3) % 4, 1))
-        self.wires.arrived(t[3], self.block((q + 1) % 4, 0))
-        self.wires.arrived(t[4], self.block((q + 2) % 4, 0))
-        self.wires.arrived(t[5], self.block((q + 2) % 4, 1))
+        self.base = [wires.ticket() for _ in range(6)][0]
+
+    def start(self, h):
+        w, mine = self.wires, self.block(self.q, h)
+        w.send(self.base + 3 * h, mine, mine, w.step(self.axis, 1 + 2 * h))
+        w.send(self.base + 3 * h + 1, mine, mine, w.step(self.axis, 3 + 2 * h))
+
+    def forward(self, h):
+        w, piece = self.wires, self.block((self.q + 3 + 2 * h) % 4, h)
+        w.arrived(self.base + 3 * h, piece)
+        w.send(self.base + 3 * h + 2, piece, piece, w.step(self.axis, 1 + 2 * h))
+
+    def end(self, h):
+        w, q = self.wires, self.q
+        w.arrived(self.base + 3 * h + 1, self.block((q + 1 + 2 * h) % 4, h))
+        w.arrived(self.base + 3 * h + 2, self.block((q + 2) % 4, h))
 
 
 class RingReduce:
-    def __init__(self, wires, axis, block, near, far_left, far_right):
+    def __init__(self, wires, axis, block, near, direct, relay):
         self.wires, self.axis, self.block = wires, axis, block
-        self.near, self.far = near, (far_left, far_right)
+        self.near, self.direct, self.relay = near, direct, relay
         self.q = getattr(wires, axis)
-        self.tickets = [wires.ticket() for _ in range(6)]
-
-    def start(self):
-        w, t, q = self.wires, self.tickets, self.q
-        right, left = w.step(self.axis, 1), w.step(self.axis, 3)
-        w.send(t[0], self.block((q + 2) % 4, 0), self.near.at[0], right)
-        w.send(t[1], self.block((q + 2) % 4, 1), self.near.at[1], left)
-        w.send(t[2], self.block((q + 1) % 4, 1), self.far[0].at[1], right)
-        w.send(t[3], self.block((q + 3) % 4, 0), self.far[1].at[0], left)
-
-    def forward(self):
-        w, t, q = self.wires, self.tickets, self.q
-        right, left = w.step(self.axis, 1), w.step(self.axis, 3)
-        for half, target, other in ((0, (q + 1) % 4, right), (1, (q + 3) % 4, left)):
-            w.arrived(t[half], self.near.at[half])
-            own = self.block(target, half)[...].astype(jnp.float32)
-            self.near[half] = (self.near[half].astype(jnp.float32) + own).astype(jnp.bfloat16)
-            w.send(t[4 + half], self.near.at[half], self.far[half].at[half], other)
-
-    def end(self, out):
-        w, t, q = self.wires, self.tickets, self.q
-        w.arrived(t[2], self.far[0].at[1])
-        w.arrived(t[3], self.far[1].at[0])
-        w.arrived(t[4], self.far[0].at[0])
-        w.arrived(t[5], self.far[1].at[1])
-        for half in range(2):
-            total = self.block(q, half)[...].astype(jnp.float32)
-            total = total + self.far[0][half].astype(jnp.float32)
-            total = total + self.far[1][half].astype(jnp.float32)
-            out[half] = total.astype(out.dtype)
+        self.base = [wires.ticket() for _ in range(6)][0]
+
+    def start(self, h):
+        w, q, t = self.wires, self.q, self.base + 3 * h
+        w.send(t, self.block((q + 2) % 4, h), self.near.at[h], w.step(self.axis, 1 + 2 * h))
+        beyond = self.block((q + 3 + 2 * h) % 4, h)
+        w.send(t + 1, beyond, self.direct.at[h], w.step(self.axis, 3 + 2 * h))
+
+    def forward(self, h):
+        w, q, t = self.wires, self.q, self.base + 3 * h
+        w.arrived(t, self.near.at[h])
+        own = self.block((q + 1 + 2 * h) % 4, h)[...].astype(jnp.float32)
+        self.near[h] = (self.near[h].astype(jnp.float32) + own).astype(jnp.bfloat16)
+        w.send(t + 2, self.near.at[h], self.relay.at[h], w.step(self.axis, 1 + 2 * h))
+
+    def end(self, h, out):
+        w, t = self.wires, self.base + 3 * h
+        w.arrived(t + 1, self.direct.at[h])
+        w.arrived(t + 2, self.relay.at[h])
+        total = self.block(self.q, h)[...].astype(jnp.float32)
+        total = total + self.direct[h].astype(jnp.float32)
+        total = total + self.relay[h].astype(jnp.float32)
+        out[h] = total.astype(out.dtype)
 
 
 def read_links(links, chip, table, slots, place, order, inward, onward):
@@ -223,8 +206,8 @@
     links, occupancy, features, cotangent, shard, input_grad, grad,
     rows, cot_own, mask, table, slots, place, order, inward, onward,
     parts, feat, cot, blocks, regions, delta_t, stage, weight, weight_t, thin,
-    a_near, a_left, a_right, b_near, b_left, b_right, a_mid, b_mid,
-    c_near, c_left, c_right, d_near, d_left, d_right, last, from_z,
+    a_near, a_direct, a_relay, b_near, b_direct, b_relay, a_mid, b_mid,
+    c_near, c_direct, c_relay, d_near, d_direct, d_relay, last, from_z,
     halves, inbox, chip_sum, z_out, z_in, fin_out, fin_in,
     local_sem, send_sem, recv_sem,
 ):
@@ -246,10 +229,10 @@
     first_b = RingGather(w, "y", lambda q, h: parts.at[h, x, q, CUT:])
     last_a = RingGather(w, "y", lambda q, h: parts.at[h, :, q, :CUT])
     last_b = RingGather(w, "x", lambda q, h: parts.at[h, q, :, CUT:])
-    sum_a = RingReduce(w, "y", lambda q, h: parts.at[h, :, q, :CUT], a_near, a_left, a_right)
-    sum_b = RingReduce(w, "x", lambda q, h: parts.at[h, q, :, CUT:], b_near, b_left, b_right)
-    end_a = RingReduce(w, "x", lambda q, h: a_mid.at[h, q], c_near, c_left, c_right)
-    end_b = RingReduce(w, "y", lambda q, h: b_mid.at[h, q], d_near, d_left, d_right)
+    sum_a = RingReduce(w, "y", lambda q, h: parts.at[h, :, q, :CUT], a_near, a_direct, a_relay)
+    sum_b = RingReduce(w, "x", lambda q, h: parts.at[h, q, :, CUT:], b_near, b_direct, b_relay)
+    end_a = RingReduce(w, "x", lambda q, h: a_mid.at[h, q], c_near, c_direct, c_relay)
+    end_b = RingReduce(w, "y", lambda q, h: b_mid.at[h, q], d_near, d_direct, d_relay)
     t_out, t_fin = w.ticket(), w.ticket()
     t_core = [w.ticket() for _ in range(live)]
     t_chip = [w.ticket() for _ in range(live)]
@@ -261,42 +244,53 @@
     lane = lax.broadcasted_iota(jnp.int32, turned.shape, 1)
     rows[:rows_of] = jnp.where(lane < width, turned, 0.0).astype(jnp.bfloat16)
     w.met(w.everyone())
+    rounds = (z, 1 - z)
     w.send(t_z, rows, parts.at[z, x, y], w.at(z=1 - z))
     w.send(t_over, features.at[0], feat.at[me], to_over)
-    w.send(t_beside, features.at[0], feat.at[me], to_beside)
     keep = [
         pltpu.make_async_copy(rows, parts.at[z, x, y], local_sem.at[0]),
         pltpu.make_async_copy(features.at[0], feat.at[me], local_sem.at[1]),
     ]
     for copy in keep:
         copy.start()
+    keep[0].wait()
+    first_a.start(z)
+    first_b.start(z)
+    w.send(t_beside, features.at[0], feat.at[me], to_beside)
     read_links(links, chip, table, slots, place, order, inward, onward)
-    keep[0].wait()
+    first_a.forward(z)
+    first_b.forward(z)
     w.arrived(t_z, parts.at[1 - z, x, y])
-    first_a.start()
-    first_b.start()
+    first_a.start(1 - z)
+    first_b.start(1 - z)
     for s in range(spatial):
         for n in range(capacity):
             some = lanes_from(cotangent[0, n].astype(jnp.float32), s * width)
             cot_own[s, n] = some.T[:width].astype(jnp.bfloat16)
     cot[me] = cot_own[me]
     w.send(c_beside, cot_own.at[beside], cot.at[me], to_beside)
+    first_a.end(z)
+    first_b.end(z)
+    last_a.start(z)
+    last_b.start(z)
+    first_a.forward(1 - z)
+    first_b.forward(1 - z)
     held = occupancy[0].astype(jnp.float32)
     held = jnp.concatenate([held] * (LANES // group), axis=0).T
     for s in range(group):
         mask[s] = jnp.broadcast_to(held[:, s : s + 1], (voxels, LANES))
-    first_a.forward()
-    first_b.forward()
-    first_a.end()
-    first_b.end()
-    last_a.start()
-    last_b.start()
+    last_a.forward(z)
+    last_b.forward(z)
+    first_a.end(1 - z)
+    first_b.end(1 - z)
+    last_a.start(1 - z)
+    last_b.start(1 - z)
     w.arrived(t_over, feat.at[over])
     w.send(t_across, feat.at[over], feat.at[over], to_beside)
     w.send(c_over, cot_own.at[over], cot.at[me], to_over)
     w.send(c_across, cot_own.at[across], cot.at[me], to_across)
-    last_a.forward()
-    last_b.forward()
+    last_a.forward(1 - z)
+    last_b.forward(1 - z)
     keep[1].wait()
     w.arrived(t_beside, feat.at[beside])
     w.arrived(t_across, feat.at[across])
@@ -307,8 +301,9 @@
         blocks[r] = (field * full).reshape(64, 8, channels)
     blocks[live] = jnp.zeros((64, 8, channels), jnp.float32)
     fill_regions(table, blocks, regions, live)
-    last_a.end()
-    last_b.end()
+    for h in rounds:
+        last_a.end(h)
+        last_b.end(h)
     for d in range(32):
         stage[rows_of * d : rows_of * d + CHUNK] = parts[d % 2, d // 8, d // 2 % 4].astype(
             jnp.float32
@@ -355,8 +350,9 @@
         parts[d % 2, d // 8, d // 2 % 4] = stage[rows_of * d : rows_of * d + CHUNK].astype(
             jnp.bfloat16
         )
-    sum_a.start()
-    sum_b.start()
+    for h in rounds[::-1]:
+        sum_a.start(h)
+        sum_b.start(h)
 
     thin[live] = jnp.zeros((64, 8, LANES), jnp.float32)
     narrow = regions.at[:, :, :, :, :LANES]
@@ -386,25 +382,36 @@
         z_out[j] = value.astype(jnp.bfloat16)
         w.send(t_chip[j], z_out.at[j], z_in.at[j], to_over)
 
+    first, second = 1 - z, z
     back_block(0)
+    sum_a.forward(first)
+    sum_b.forward(first)
     back_block(1)
     join(0)
-    sum_a.forward()
-    sum_b.forward()
+    sum_a.forward(second)
+    sum_b.forward(second)
     back_block(2)
     join(1)
+    sum_a.end(first, a_mid)
+    sum_b.end(first, b_mid)
+    end_a.start(first)
+    end_b.start(first)
     back_block(3)
     join(2)
-    sum_a.end(a_mid)
-    sum_b.end(b_mid)
-    end_a.start()
-    end_b.start()
+    sum_a.end(second, a_mid)
+    sum_b.end(second, b_mid)
+    end_a.start(second)
+    end_b.start(second)
+    end_a.forward(first)
+    end_b.forward(first)
     join(3)
-    end_a.forward()
-    end_b.forward()
-    end_a.end(last.at[:, :CUT])
-    end_b.end(last.at[:, CUT:])
+    end_a.end(first, last.at[:, :CUT])
+    end_b.end(first, last.at[:, CUT:])
     w.send(t_out, last.at[1 - z], from_z, w.at(z=1 - z))
+    end_a.forward(second)
+    end_b.forward(second)
+    end_a.end(second, last.at[:, :CUT])
+    end_b.end(second, last.at[:, CUT:])
     for j in range(live):
         w.arrived(t_chip[j], z_in.at[j])
 

time: 91.7 us -> 94.9 us (1.035); the launches traced: 91.5 us -> 93.7 us
  Pallas kernels: 87.1 us -> 89.2 us
    pallas_call x1, Pallas kernels: 87.1 us -> 89.2 us  [step_call(): pl.pallas_call(step_kernel, out_shape=(jax.ShapeDtypeStruct(features.shap...]
where the time goes in v5:
time: 94.9 us; the launch traced here: 93.7 us
  Pallas kernels  89.2 us (94%)
  local copies, waits for them, and re-layouts  2.1 us (2%)
  other arithmetic  1.67 us (2%)
    pallas_call x1, Pallas kernels, step_call(): pl.pallas_call(step_kernel, out_shape=(jax.ShapeDtypeStruct(features.shap...  89.2 us
    unnamed x5, local copies, waits for them, and re-layouts  2.1 us

profile of v5, /device:TPU:1, one launch (start us, length us, event | category | flops | bytes accessed | tf_op | source)
XLA Modules:
  0.0 93.7 jit_solution(16338152416334465115)
XLA Ops:
  0.6 0.0 copy-start
  0.6 0.0 copy-start.1
  0.7 89.2 %shard_map.94 = (bf16[1,2,512,384]{3,2,1,0:T(8,128)(2,1)}, f32[128,384]{1,0:T(8,128)}) custom-call(s32[1,8,27]{2,1,0:T(8,128)} %links.1, s32[1,8,512]{2,1,0:T(8,128)} %occupancy.1, bf16[1,2,512,384]{3,2,1,0:T(8,128)(2,1)} %features.1, bf16[1,2,512,384]{3,2,1,0:T(8,128)(2,1)} %cotangent.1, bf16[324,384]{1,0:T(8,128)(2,1)} %shard.1), custom_call_target="tpu_custom_call" | custom-call | flops 16307453952 | bytes 10000000 | tf_op jit(solution)/shard_map/pallas_call | solution.py:464
  89.9 0.0 copy-done
  89.9 0.0 copy-done.1
  89.9 1.7 %fusion = (f32[324,96]{0,1:T(8,128)}, f32[324,96]{0,1:T(8,128)}) fusion(f32[324,96]{0,1:T(8,128)S(1)} %copy-done, f32[128,384]{1,0:T(8,128)} %get-tuple-element.6, f32[324,96]{0,1:T(8,128)S(1)} %copy-done.1), kind=kLoop, calls=%fused_computation.1 | loop fusion | flops 248832 | bytes 622080 | tf_op jit(solution)/shard_map/transpose | solution.py:524
  91.6 2.1 %copy.11 = bf16[1,2,512,384]{3,2,1,0:T(8,128)(2,1)} copy(bf16[1,2,512,384]{3,2,1,0:T(8,128)(2,1)} %get-tuple-element.12) | data formatting | bytes 1572864
Async XLA Ops:
  0.6 89.3 %copy-start = (f32[324,96]{0,1:T(8,128)S(1)}, f32[324,96]{0,1:T(8,128)}, u32[]{:S(2)}) copy-start(f32[324,96]{0,1:T(8,128)} %param.13) | copy-start | bytes 373252
  0.6 89.3 %copy-start.1 = (f32[324,96]{0,1:T(8,128)S(1)}, f32[324,96]{0,1:T(8,128)}, u32[]{:S(2)}) copy-start(f32[324,96]{0,1:T(8,128)} %param.12) | copy-start | bytes 373252

commit v6 on v4

--- a/solution.py
+++ b/solution.py
@@ -222,7 +222,7 @@
 def step_kernel(
     links, occupancy, features, cotangent, shard, input_grad, grad,
     rows, cot_own, mask, table, slots, place, order, inward, onward,
-    parts, feat, cot, blocks, regions, delta_t, stage, weight, weight_t, thin,
+    parts, feat, cot, blocks, regions, delta_t, stage, weight, weight_t, thin, pre_all,
     a_near, a_left, a_right, b_near, b_left, b_right, a_mid, b_mid,
     c_near, c_left, c_right, d_near, d_left, d_right, last, from_z,
     halves, inbox, chip_sum, z_out, z_in, fin_out, fin_in,
@@ -270,27 +270,27 @@
     ]
     for copy in keep:
         copy.start()
-    read_links(links, chip, table, slots, place, order, inward, onward)
     keep[0].wait()
     w.arrived(t_z, parts.at[1 - z, x, y])
     first_a.start()
     first_b.start()
+    read_links(links, chip, table, slots, place, order, inward, onward)
+    first_a.forward()
+    first_b.forward()
     for s in range(spatial):
         for n in range(capacity):
             some = lanes_from(cotangent[0, n].astype(jnp.float32), s * width)
             cot_own[s, n] = some.T[:width].astype(jnp.bfloat16)
     cot[me] = cot_own[me]
     w.send(c_beside, cot_own.at[beside], cot.at[me], to_beside)
+    first_a.end()
+    first_b.end()
+    last_a.start()
+    last_b.start()
     held = occupancy[0].astype(jnp.float32)
     held = jnp.concatenate([held] * (LANES // group), axis=0).T
     for s in range(group):
         mask[s] = jnp.broadcast_to(held[:, s : s + 1], (voxels, LANES))
-    first_a.forward()
-    first_b.forward()
-    first_a.end()
-    first_b.end()
-    last_a.start()
-    last_b.start()
     w.arrived(t_over, feat.at[over])
     w.send(t_across, feat.at[over], feat.at[over], to_beside)
     w.send(c_over, cot_own.at[over], cot.at[me], to_over)
@@ -317,9 +317,6 @@
         some = stage[pl.ds(k, channels, stride=27), :]
         weight[k * channels : (k + 1) * channels] = some.astype(jnp.bfloat16)
         weight_t[:, k * channels : (k + 1) * channels] = some.T[:width].astype(jnp.bfloat16)
-    w.arrived(c_over, cot.at[over])
-    w.arrived(c_beside, cot.at[beside])
-    w.arrived(c_across, cot.at[across])
 
     def forward_block(r):
         pre = jnp.zeros((width, voxels), jnp.float32)
@@ -329,6 +326,10 @@
             pre = pre + lax.dot_general(
                 lhs, field, (((1,), (1,)), ((), ())), preferred_element_type=jnp.float32
             )
+        pre_all[r] = pre
+
+    def delta_block(r):
+        pre = pre_all[r]
         gate = jax.nn.sigmoid(pre)
         value = cot[slots[r] // capacity, slots[r] % capacity].astype(jnp.float32)
         value = value * occupancy[0, pl.ds(slots[r], 1)].astype(jnp.float32)
@@ -341,6 +342,11 @@
 
     for r in range(live):
         forward_block(r)
+    w.arrived(c_over, cot.at[over])
+    w.arrived(c_beside, cot.at[beside])
+    w.arrived(c_across, cot.at[across])
+    for r in range(live):
+        delta_block(r)
     for k in range(27):
         field = jnp.concatenate(
             [shifted_rows(regions, r, k, channels) for r in range(live)], axis=0
@@ -482,6 +488,7 @@
             buffer(27 * channels, LANES),
             buffer(channels // spatial, 27 * channels),
             wide(live + 1, 64, 8, LANES),
+            wide(live, channels // spatial, voxels),
         ]
         + ring(4, CUT)
         + ring(4, rest)

time: 91.7 us -> 89.4 us (0.975)
  Pallas kernels: 87.1 us -> 84.5 us
    pallas_call x1, Pallas kernels: 87.1 us -> 84.5 us  [step_call(): pl.pallas_call(step_kernel, out_shape=(jax.ShapeDtypeStruct(features.shap...]
where the time goes in v6:
time: 89.4 us; the launch traced here: 89 us
  Pallas kernels  84.5 us (95%)
  local copies, waits for them, and re-layouts  2.1 us (2%)
  other arithmetic  1.67 us (2%)
    pallas_call x1, Pallas kernels, step_call(): pl.pallas_call(step_kernel, out_shape=(jax.ShapeDtypeStruct(features.shap...  84.5 us
    unnamed x5, local copies, waits for them, and re-layouts  2.1 us

profile of v6, /device:TPU:1, one launch (start us, length us, event | category | flops | bytes accessed | tf_op | source)
XLA Modules:
  0.0 89.0 jit_solution(6210672037050152851)
XLA Ops:
  0.6 0.0 copy-start
  0.6 0.0 copy-start.1
  0.7 84.5 %shard_map.94 = (bf16[1,2,512,384]{3,2,1,0:T(8,128)(2,1)}, f32[128,384]{1,0:T(8,128)}) custom-call(s32[1,8,27]{2,1,0:T(8,128)} %links.1, s32[1,8,512]{2,1,0:T(8,128)} %occupancy.1, bf16[1,2,512,384]{3,2,1,0:T(8,128)(2,1)} %features.1, bf16[1,2,512,384]{3,2,1,0:T(8,128)(2,1)} %cotangent.1, bf16[324,384]{1,0:T(8,128)(2,1)} %shard.1), custom_call_target="tpu_custom_call" | custom-call | flops 16307453952 | bytes 10000000 | tf_op jit(solution)/shard_map/pallas_call | solution.py:463
  85.2 0.0 copy-done
  85.2 0.0 copy-done.1
  85.2 1.7 %fusion = (f32[324,96]{0,1:T(8,128)}, f32[324,96]{0,1:T(8,128)}) fusion(f32[324,96]{0,1:T(8,128)S(1)} %copy-done, f32[128,384]{1,0:T(8,128)} %get-tuple-element.6, f32[324,96]{0,1:T(8,128)S(1)} %copy-done.1), kind=kLoop, calls=%fused_computation.1 | loop fusion | flops 248832 | bytes 622080 | tf_op jit(solution)/shard_map/transpose | solution.py:524
  86.9 2.1 %copy.11 = bf16[1,2,512,384]{3,2,1,0:T(8,128)(2,1)} copy(bf16[1,2,512,384]{3,2,1,0:T(8,128)(2,1)} %get-tuple-element.12) | data formatting | bytes 1572864
Async XLA Ops:
  0.6 84.5 %copy-start = (f32[324,96]{0,1:T(8,128)S(1)}, f32[324,96]{0,1:T(8,128)}, u32[]{:S(2)}) copy-start(f32[324,96]{0,1:T(8,128)} %param.13) | copy-start | bytes 373252
  0.6 84.5 %copy-start.1 = (f32[324,96]{0,1:T(8,128)S(1)}, f32[324,96]{0,1:T(8,128)}, u32[]{:S(2)}) copy-start(f32[324,96]{0,1:T(8,128)} %param.12) | copy-start | bytes 373252

commit v7 on v6

--- a/solution.py
+++ b/solution.py
@@ -240,7 +240,9 @@
     across = (1 - chip) * 2 + 1 - core
     to_over, to_beside = w.at(chip=1 - chip), w.at(core=1 - core)
     to_across = w.at(chip=1 - chip, core=1 - core)
-    t_z, t_over, t_beside, t_across = (w.ticket() for _ in range(4))
+    t_z, t_beside = w.ticket(), w.ticket()
+    t_over = [w.ticket() for _ in range(capacity)]
+    t_across = [w.ticket() for _ in range(capacity)]
     c_over, c_beside, c_across = (w.ticket() for _ in range(3))
     first_a = RingGather(w, "x", lambda q, h: parts.at[h, q, y, :CUT])
     first_b = RingGather(w, "y", lambda q, h: parts.at[h, x, q, CUT:])
@@ -262,7 +264,8 @@
     rows[:rows_of] = jnp.where(lane < width, turned, 0.0).astype(jnp.bfloat16)
     w.met(w.everyone())
     w.send(t_z, rows, parts.at[z, x, y], w.at(z=1 - z))
-    w.send(t_over, features.at[0], feat.at[me], to_over)
+    for n in range(capacity):
+        w.send(t_over[n], features.at[0, n], feat.at[me, n], to_over)
     w.send(t_beside, features.at[0], feat.at[me], to_beside)
     keep = [
         pltpu.make_async_copy(rows, parts.at[z, x, y], local_sem.at[0]),
@@ -277,29 +280,31 @@
     read_links(links, chip, table, slots, place, order, inward, onward)
     first_a.forward()
     first_b.forward()
+    first_a.end()
+    first_b.end()
+    last_a.start()
+    last_b.start()
     for s in range(spatial):
         for n in range(capacity):
             some = lanes_from(cotangent[0, n].astype(jnp.float32), s * width)
             cot_own[s, n] = some.T[:width].astype(jnp.bfloat16)
     cot[me] = cot_own[me]
     w.send(c_beside, cot_own.at[beside], cot.at[me], to_beside)
-    first_a.end()
-    first_b.end()
-    last_a.start()
-    last_b.start()
+    for n in range(capacity):
+        w.arrived(t_over[n], feat.at[over, n])
+        w.send(t_across[n], feat.at[over, n], feat.at[over, n], to_beside)
+    w.send(c_over, cot_own.at[over], cot.at[me], to_over)
+    w.send(c_across, cot_own.at[across], cot.at[me], to_across)
+    last_a.forward()
+    last_b.forward()
     held = occupancy[0].astype(jnp.float32)
     held = jnp.concatenate([held] * (LANES // group), axis=0).T
     for s in range(group):
         mask[s] = jnp.broadcast_to(held[:, s : s + 1], (voxels, LANES))
-    w.arrived(t_over, feat.at[over])
-    w.send(t_across, feat.at[over], feat.at[over], to_beside)
-    w.send(c_over, cot_own.at[over], cot.at[me], to_over)
-    w.send(c_across, cot_own.at[across], cot.at[me], to_across)
-    last_a.forward()
-    last_b.forward()
     keep[1].wait()
     w.arrived(t_beside, feat.at[beside])
-    w.arrived(t_across, feat.at[across])
+    for n in range(capacity):
+        w.arrived(t_across[n], feat.at[across, n])
 
     for r in range(live):
         full = jnp.concatenate([mask[slots[r]]] * (channels // LANES), axis=1)
@@ -357,12 +362,11 @@
         )
         stage[pl.ds(k, channels, stride=27), :] = part.T
     w.finish()
-    for d in range(32):
-        parts[d % 2, d // 8, d // 2 % 4] = stage[rows_of * d : rows_of * d + CHUNK].astype(
-            jnp.bfloat16
-        )
-    sum_a.start()
-    sum_b.start()
+    for ring, low, high in ((sum_a, 0, CUT), (sum_b, CUT, CHUNK)):
+        for d in range(32):
+            piece = stage[rows_of * d + low : rows_of * d + high]
+            parts[d % 2, d // 8, d // 2 % 4, low:high] = piece.astype(jnp.bfloat16)
+        ring.start()
 
     thin[live] = jnp.zeros((64, 8, LANES), jnp.float32)
     narrow = regions.at[:, :, :, :, :LANES]
@@ -444,7 +448,7 @@
     capacity, voxels, channels = features.shape[1:]
     spatial, half = group // capacity, voxels // 2
     rest = CHUNK - CUT
-    copies = 8 * 6 + 9 + 2 * live
+    copies = 8 * 6 + 7 + 2 * capacity + 2 * live
 
     def buffer(*shape):
         return pltpu.VMEM(shape, jnp.bfloat16)

time: 89.4 us -> 89.4 us (level)
  no operation moved by 1% of the time
where the time goes in v7:
time: 89.4 us; the launch traced here: 88.5 us
  Pallas kernels  84.1 us (94%)
  local copies, waits for them, and re-layouts  2.1 us (2%)
  other arithmetic  1.67 us (2%)
    pallas_call x1, Pallas kernels, step_call(): pl.pallas_call(step_kernel, out_shape=(jax.ShapeDtypeStruct(features.shap...  84.1 us
    unnamed x5, local copies, waits for them, and re-layouts  2.1 us

profile of v7, /device:TPU:1, one launch (start us, length us, event | category | flops | bytes accessed | tf_op | source)
XLA Modules:
  0.0 88.5 jit_solution(3759595315521584266)
XLA Ops:
  0.6 0.0 copy-start
  0.6 0.0 copy-start.1
  0.7 84.1 %shard_map.94 = (bf16[1,2,512,384]{3,2,1,0:T(8,128)(2,1)}, f32[128,384]{1,0:T(8,128)}) custom-call(s32[1,8,27]{2,1,0:T(8,128)} %links.1, s32[1,8,512]{2,1,0:T(8,128)} %occupancy.1, bf16[1,2,512,384]{3,2,1,0:T(8,128)(2,1)} %features.1, bf16[1,2,512,384]{3,2,1,0:T(8,128)(2,1)} %cotangent.1, bf16[324,384]{1,0:T(8,128)(2,1)} %shard.1), custom_call_target="tpu_custom_call" | custom-call | flops 16307453952 | bytes 10000000 | tf_op jit(solution)/shard_map/pallas_call | solution.py:467
  84.8 0.0 copy-done
  84.8 0.0 copy-done.1
  84.8 1.7 %fusion = (f32[324,96]{0,1:T(8,128)}, f32[324,96]{0,1:T(8,128)}) fusion(f32[324,96]{0,1:T(8,128)S(1)} %copy-done, f32[128,384]{1,0:T(8,128)} %get-tuple-element.6, f32[324,96]{0,1:T(8,128)S(1)} %copy-done.1), kind=kLoop, calls=%fused_computation.1 | loop fusion | flops 248832 | bytes 622080 | tf_op jit(solution)/shard_map/transpose | solution.py:528
  86.4 2.1 %copy.11 = bf16[1,2,512,384]{3,2,1,0:T(8,128)(2,1)} copy(bf16[1,2,512,384]{3,2,1,0:T(8,128)(2,1)} %get-tuple-element.12) | data formatting | bytes 1572864
Async XLA Ops:
  0.6 84.1 %copy-start = (f32[324,96]{0,1:T(8,128)S(1)}, f32[324,96]{0,1:T(8,128)}, u32[]{:S(2)}) copy-start(f32[324,96]{0,1:T(8,128)} %param.13) | copy-start | bytes 373252
  0.6 84.1 %copy-start.1 = (f32[324,96]{0,1:T(8,128)S(1)}, f32[324,96]{0,1:T(8,128)}, u32[]{:S(2)}) copy-start(f32[324,96]{0,1:T(8,128)} %param.12) | copy-start | bytes 373252
